TPU v7x, 512 devices: a whole 4x8x8 slice. The times are simulated.
512 devices in a mesh: orb: 32 (over y, x), aux: 16 (over z, core).
Axes of the slice: x: 4, y: 8, z: 8, core: 2. Of those that a mesh axis runs over, the one named last changes fastest.
Arguments:
- three_center: bfloat16 [4096, 18432], P('orb', 'aux'), may hold values from -6 to 6
- metric_tensor: bfloat16 [4096, 18432], P('orb', 'aux'), may hold values from -0.046875 to 0.046875
- density: bfloat16 [4096, 144], P('orb'), may hold values from -0.5 to 0.5
- pattern: int32 [256, 9], P('orb'), may hold values 0 or 1
- block_size: int32 [256], replicated, may hold values from 8 to 16
Outputs:
- exchange: bfloat16 [4096, 144], P(('orb', 'aux'))
All inputs are finite; a program needn't handle non-finite values. No bound on the sum of `pattern` on one device may be relied on, other than what follows from the above.
Results may differ from a plain program's by a relative error of at most 0.0049.
Values may be sent and summed in bfloat16 or wider, within the bound.
No kernel may reach another device: no remote copies, remote signals or barrier semaphores. Data moves between devices by JAX's collectives and lax.ppermute only.
A program may use at most 64 MiB of HBM per device.

v0:
```python
import jax
import jax.numpy as jnp
from jax import lax
from jax.sharding import PartitionSpec as P

BS = 16


def extended(x, sides, width):
    for axis, dim in sides:
        peers, length = (lax.axis_size(axis), x.shape[dim])
        up = [(i, (i + 1) % peers) for i in range(peers)]
        down = [(j, i) for i, j in up]
        last = lax.slice_in_dim(x, length - width, length, axis=dim)
        first = lax.slice_in_dim(x, 0, width, axis=dim)
        before = lax.ppermute(last, axis, up)
        after = lax.ppermute(first, axis, down)
        x = jnp.concatenate([before, x, after], axis=dim)
    return x


def slot_shift(values, offset, along):
    length = values.shape[along]
    if offset == 0:
        return values
    zero_shape = list(values.shape)
    zero_shape[along] = abs(offset)
    zeros = jnp.zeros(zero_shape, values.dtype)
    if offset > 0:
        return jnp.concatenate(
            [zeros, lax.slice_in_dim(values, 0, length - offset, axis=along)], axis=along
        )
    return jnp.concatenate(
        [lax.slice_in_dim(values, -offset, length, axis=along), zeros], axis=along
    )


def on_device(three_center, metric_tensor, density, pattern, block_size):
    atom_count = pattern.shape[0]
    band_slots = pattern.shape[1]
    band_half = (band_slots - 1) // 2
    band_width = band_slots * BS
    local_funcs = three_center.shape[1] // band_width
    total_atoms = atom_count * lax.axis_size("orb")
    first_atom = lax.axis_index("orb") * atom_count
    wrapped = jnp.concatenate(
        [block_size[total_atoms - band_half :], block_size, block_size[:band_half]]
    )
    beside_all = lax.dynamic_slice_in_dim(wrapped, first_atom, atom_count + 2 * band_half)
    func_ids = jnp.arange(BS, dtype=jnp.int32)
    is_live = func_ids[None, :] < beside_all[:, None]
    col_live = jnp.stack([is_live[slot : slot + atom_count] for slot in range(band_slots)], axis=1)
    row_live = is_live[band_half : band_half + atom_count]
    kept = row_live[:, :, None, None] & (pattern[:, None, :, None] > 0) & col_live[:, None, :, :]
    kept = kept.reshape(atom_count * BS, band_width)
    zero_value = jnp.zeros((), jnp.bfloat16)
    tensor_live = jnp.where(
        kept[:, None, :], three_center.reshape(atom_count * BS, local_funcs, band_width), zero_value
    )
    metric_live = jnp.where(
        kept[:, None, :],
        metric_tensor.reshape(atom_count * BS, local_funcs, band_width),
        zero_value,
    )
    density_live = jnp.where(kept, density, zero_value)
    density_ext = extended(
        density_live.reshape(atom_count, BS * band_width), (("orb", 0),), band_half
    )
    density_ext = density_ext.reshape(atom_count + 2 * band_half, BS, band_slots, BS)
    pieces = [
        slot_shift(density_ext[slot : slot + atom_count], slot - band_half, 2)
        for slot in range(band_slots)
    ]
    spread = jnp.stack(pieces, axis=1).reshape(atom_count, band_width, band_width)
    spread_wide = jnp.pad(spread, ((0, 0), (0, 0), (band_half * BS, band_half * BS)))
    left_rows = tensor_live.reshape(atom_count, BS * local_funcs, band_width)
    metric_rows = metric_live.reshape(atom_count, BS, local_funcs, band_width)
    metric_ext = extended(
        metric_rows.reshape(atom_count, BS * local_funcs * band_width), (("orb", 0),), band_half
    )
    metric_ext = metric_ext.reshape(atom_count + 2 * band_half, BS, local_funcs * band_width)
    slot_terms = []
    for slot in range(band_slots):
        spread_slot = spread_wide[:, :, slot * BS : slot * BS + band_width]
        shifted = jnp.einsum(
            "ark,akn->arn", left_rows, spread_slot, preferred_element_type=jnp.float32
        ).astype(jnp.bfloat16)
        shifted = shifted.reshape(atom_count, BS, local_funcs * band_width)
        partner = metric_ext[slot : slot + atom_count]
        slot_terms.append(
            jnp.einsum("amc,aqc->amq", shifted, partner, preferred_element_type=jnp.float32)
        )
    partial_sum = jnp.stack(slot_terms, axis=2) * pattern.astype(jnp.float32)[:, None, :, None]
    partial_sum = partial_sum.reshape(atom_count * BS, band_width)
    summed = lax.psum(partial_sum, "aux")
    row_share = atom_count * BS // lax.axis_size("aux")
    summed = lax.dynamic_slice_in_dim(summed, lax.axis_index("aux") * row_share, row_share, 0)
    return summed.astype(jnp.bfloat16)


def solution(mesh):
    placed = (P("orb", "aux"), P("orb", "aux"), P("orb", None), P("orb", None), P())
    return jax.shard_map(
        on_device, mesh=mesh, in_specs=placed, out_specs=P(("orb", "aux"), None), check_vma=False
    )
```

profile of v0, /device:TPU:1, one launch (start us, length us, event | category | flops | bytes accessed | tf_op | source)
XLA Modules:
  0.0 147.6 jit_solution(6016969920870865605)
XLA Ops:
  0.0 0.8 fusion.56
  0.8 0.8 pad_add_fusion
  3.3 0.8 broadcast_select_fusion.2
  4.4 3.9 %collective-permute-start = (bf16[4,2304]{1,0:T(4,128)(2,1)S(1)}, bf16[4,2304]{1,0:T(4,128)(2,1)S(1)}, u32[]{:S(2)}, u32[]{:S(2)}) collective-permute-start(bf16[4,2304]{1,0:T(4,128)(2,1)S(1)} %slice.235), channel_id=1, source_target_pairs={{0,16},{16,32},{32,48},{48,64},{64,80},{80,96},{96,112},{112,128},... | collective-permute-start | bytes 55304 | tf_op jit(solution)/shard_map/ppermute | solution.py:16
  8.5 0.7 slice.249
  9.2 6.1 %collective-permute-start.1 = (bf16[4,2304]{1,0:T(4,128)(2,1)}, bf16[4,2304]{1,0:T(4,128)(2,1)}, u32[]{:S(2)}, u32[]{:S(2)}) collective-permute-start(bf16[4,2304]{1,0:T(4,128)(2,1)} %slice.249), channel_id=1, source_target_pairs={{16,0},{32,16},{48,32},{64,48},{80,64},{96,80},{112,96},{128,112},... | collective-permute-start | bytes 55304 | tf_op jit(solution)/shard_map/ppermute | solution.py:17
  15.3 1.2 copy.116
  16.9 1.1 slice.264
  18.0 1.9 %collective-permute-start.2 = (bf16[4,18432]{1,0:T(4,128)(2,1)}, bf16[4,18432]{1,0:T(4,128)(2,1)}, u32[]{:S(2)}, u32[]{:S(2)}) collective-permute-start(bf16[4,18432]{1,0:T(4,128)(2,1)} %slice.264), channel_id=1, source_target_pairs={{0,16},{16,32},{32,48},{48,64},{64,80},{80,96},{96,112},{112,128},... | collective-permute-start | bytes 442376 | tf_op jit(solution)/shard_map/ppermute | solution.py:16
  20.2 1.1 slice.278
  21.2 6.7 %collective-permute-start.3 = (bf16[4,18432]{1,0:T(4,128)(2,1)}, bf16[4,18432]{1,0:T(4,128)(2,1)}, u32[]{:S(2)}, u32[]{:S(2)}) collective-permute-start(bf16[4,18432]{1,0:T(4,128)(2,1)} %slice.278), channel_id=1, source_target_pairs={{16,0},{32,16},{48,32},{64,48},{80,64},{96,80},{112,96},{128,112},... | collective-permute-start | bytes 442376 | tf_op jit(solution)/shard_map/ppermute | solution.py:17
  30.2 1.2 broadcast_in_dim.45
  31.5 0.9 copy.111
  33.7 1.9 %slice.240 = bf16[8,16,9,16]{3,2,1,0:T(8,128)(2,1)} reshape(bf16[8,2304]{1,0:T(8,128)(2,1)} %get-tuple-element.25) | data formatting | bytes 73728 | tf_op jit(solution)/shard_map/slice | solution.py:71
  35.7 1.1 slice.305
  37.5 1.9 %slice.243 = bf16[8,16,9,16]{3,2,1,0:T(8,128)(2,1)} reshape(bf16[8,2304]{1,0:T(8,128)(2,1)} %get-tuple-element.26) | data formatting | bytes 73728 | tf_op jit(solution)/shard_map/slice | solution.py:71
  39.4 1.1 slice.308
  41.3 1.9 %slice.246 = bf16[8,16,9,16]{3,2,1,0:T(8,128)(2,1)} reshape(bf16[8,2304]{1,0:T(8,128)(2,1)} %get-tuple-element.23) | data formatting | bytes 73728 | tf_op jit(solution)/shard_map/slice | solution.py:71
  43.2 1.1 slice.309
  44.3 0.8 copy.156
  45.1 0.7 constant_dynamic-update-slice_fusion.9
  46.5 1.9 %slice.251 = bf16[8,16,9,16]{3,2,1,0:T(8,128)(2,1)} reshape(bf16[8,2304]{1,0:T(8,128)(2,1)} %get-tuple-element.22) | data formatting | bytes 73728 | tf_op jit(solution)/shard_map/slice | solution.py:71
  48.5 1.0 slice.312
  49.4 0.7 copy.157
  50.2 1.9 %slice.254 = bf16[8,16,9,16]{3,2,1,0:T(8,128)(2,1)} reshape(bf16[8,2304]{1,0:T(8,128)(2,1)} %get-tuple-element.21) | data formatting | bytes 73728 | tf_op jit(solution)/shard_map/slice | solution.py:71
  52.1 1.0 slice.314
  53.8 1.2 slice.257
  54.9 1.0 slice.316
  56.6 1.2 slice.260
  57.8 1.1 slice.318
  58.9 1.0 fusion.37
  59.9 1.0 fusion.36
  60.9 1.0 fusion.35
  62.3 3.4 %copy.112 = bf16[8,9,16,9,16]{4,3,2,1,0:T(8,128)(2,1)} copy(bf16[8,9,16,9,16]{4,2,3,1,0:T(8,128)(2,1)S(1)} %fusion.31) | data formatting | bytes 663552 | tf_op jit(solution)/shard_map/stack | solution.py:74
  65.7 5.5 %reshape.111 = bf16[8,144,144]{2,1,0:T(8,128)(2,1)S(1)} reshape(bf16[8,9,16,9,16]{4,3,2,1,0:T(8,128)(2,1)} %copy.112) | data formatting | bytes 663552 | tf_op jit(solution)/shard_map/reshape | solution.py:74
  71.6 1.0 convolution_convert_fusion.8
  72.7 1.0 convolution_convert_fusion.7
  73.7 1.0 convolution_convert_fusion.6
  76.5 1.2 copy.115
  77.6 1.2 reshape.112
  78.8 1.2 copy.120
  80.0 1.2 reshape.115
  81.1 1.2 copy.122
  82.3 1.2 reshape.116
  83.7 1.2 reshape.117
  88.1 1.2 reshape.123
  89.3 2.7 %pad_maximum_fusion = (bf16[8,18432]{1,0:T(8,128)(2,1)S(1)}, bf16[8,18432]{1,0:T(8,128)(2,1)S(1)}, bf16[8,18432]{1,0:T(8,128)(2,1)S(1)}, bf16[8,18432]{1,0:T(8,1...) fusion(bf16[4,18432]{1,0:T(4,128)(2,1)} %collective-permute-don, ...), kind=kLoop, calls=%fused_computation.70 | loop fusion | flops 4718592 | bytes 2949120 | tf_op jit(solution)/shard_map/concatenate | solution.py:18
  95.0 52.0 %psum.7 = bf16[128,144]{1,0:T(8,128)(2,1)S(1)} all-reduce(f32[128,144]{1,0:T(8,128)S(1)} %copy.140), channel_id=1, replica_groups=mesh['orb'=32,'aux'=16] {'aux'}, use_global_device_ids=true, to_apply=%region_0.1 | all-reduce | flops 18432 | bytes 110592 | tf_op jit(solution)/shard_map/psum | solution.py:95
  (121 shorter events, 19.3 us)
Async XLA Ops:
  0.0 28.0 %copy-start = (bf16[128,1152]{1,0:T(8,128)(2,1)S(1)}, bf16[128,1152]{1,0:T(8,128)(2,1)}, u32[]{:S(2)}) copy-start(bf16[128,1152]{1,0:T(8,128)(2,1)} %param.6) | copy-start | bytes 884740
  4.1 24.1 %copy-start.6 = (bf16[128,1152]{1,0:T(8,128)(2,1)S(1)}, bf16[128,1152]{1,0:T(8,128)(2,1)}, u32[]{:S(2)}) copy-start(bf16[128,1152]{1,0:T(8,128)(2,1)} %param.5) | copy-start | bytes 884740
  4.4 28.1 %collective-permute-start = (bf16[4,2304]{1,0:T(4,128)(2,1)S(1)}, bf16[4,2304]{1,0:T(4,128)(2,1)S(1)}, u32[]{:S(2)}, u32[]{:S(2)}) collective-permute-start(bf16[4,2304]{1,0:T(4,128)(2,1)S(1)} %slice.235), channel_id=1, source_target_pairs={{0,16},{16,32},{32,48},{48,64},{64,80},{80,96},{96,112},{112,128},... | collective-permute-start | bytes 55304 | tf_op jit(solution)/shard_map/ppermute | solution.py:16
  9.2 35.9 %collective-permute-start.1 = (bf16[4,2304]{1,0:T(4,128)(2,1)}, bf16[4,2304]{1,0:T(4,128)(2,1)}, u32[]{:S(2)}, u32[]{:S(2)}) collective-permute-start(bf16[4,2304]{1,0:T(4,128)(2,1)} %slice.249), channel_id=1, source_target_pairs={{16,0},{32,16},{48,32},{64,48},{80,64},{96,80},{112,96},{128,112},... | collective-permute-start | bytes 55304 | tf_op jit(solution)/shard_map/ppermute | solution.py:17
  18.0 71.4 %collective-permute-start.2 = (bf16[4,18432]{1,0:T(4,128)(2,1)}, bf16[4,18432]{1,0:T(4,128)(2,1)}, u32[]{:S(2)}, u32[]{:S(2)}) collective-permute-start(bf16[4,18432]{1,0:T(4,128)(2,1)} %slice.264), channel_id=1, source_target_pairs={{0,16},{16,32},{32,48},{48,64},{64,80},{80,96},{96,112},{112,128},... | collective-permute-start | bytes 442376 | tf_op jit(solution)/shard_map/ppermute | solution.py:16
  20.1 11.2 %copy-start.15 = (s32[8,9]{1,0:T(8,128)S(1)}, s32[8,9]{1,0:T(8,128)}, u32[]{:S(2)}) copy-start(s32[8,9]{1,0:T(8,128)} %param.8) | copy-start | bytes 868
  21.2 68.1 %collective-permute-start.3 = (bf16[4,18432]{1,0:T(4,128)(2,1)}, bf16[4,18432]{1,0:T(4,128)(2,1)}, u32[]{:S(2)}, u32[]{:S(2)}) collective-permute-start(bf16[4,18432]{1,0:T(4,128)(2,1)} %slice.278), channel_id=1, source_target_pairs={{16,0},{32,16},{48,32},{64,48},{80,64},{96,80},{112,96},{128,112},... | collective-permute-start | bytes 442376 | tf_op jit(solution)/shard_map/ppermute | solution.py:17
  46.5 7.3 %copy-start.13 = (bf16[8,2304]{1,0:T(8,128)(2,1)S(1)}, bf16[8,2304]{1,0:T(8,128)(2,1)}, u32[]{:S(2)}) copy-start(bf16[8,2304]{1,0:T(8,128)(2,1)} %get-tuple-element.20) | copy-start | bytes 110596
  46.5 10.1 %copy-start.12 = (bf16[8,2304]{1,0:T(8,128)(2,1)S(1)}, bf16[8,2304]{1,0:T(8,128)(2,1)}, u32[]{:S(2)}) copy-start(bf16[8,2304]{1,0:T(8,128)(2,1)} %get-tuple-element.19) | copy-start | bytes 110596
  57.8 4.2 %copy-start.2 = (bf16[8,1,16,9,16]{4,2,3,1,0:T(8,128)(2,1)S(1)}, bf16[8,1,16,9,16]{4,2,3,1,0:T(8,128)(2,1)}, u32[]{:S(2)}) copy-start(bf16[8,1,16,9,16]{4,2,3,1,0:T(8,128)(2,1)} %copy.111) | copy-start | bytes 110596
  57.8 4.2 %copy-start.3 = (bf16[8,16,8,16]{3,1,2,0:T(8,128)(2,1)S(1)}, bf16[8,16,8,16]{3,1,2,0:T(8,128)(2,1)}, u32[]{:S(2)}) copy-start(bf16[8,16,8,16]{3,1,2,0:T(8,128)(2,1)} %copy.157) | copy-start | bytes 98308
  57.8 4.3 %copy-start.4 = (bf16[8,16,7,16]{3,1,2,0:T(8,128)(2,1)S(1)}, bf16[8,16,7,16]{3,1,2,0:T(8,128)(2,1)}, u32[]{:S(2)}) copy-start(bf16[8,16,7,16]{3,1,2,0:T(8,128)(2,1)} %copy.158) | copy-start | bytes 86020
  57.8 4.4 %copy-start.5 = (bf16[8,16,6,16]{3,1,2,0:T(8,128)(2,1)S(1)}, bf16[8,16,6,16]{3,1,2,0:T(8,128)(2,1)}, u32[]{:S(2)}) copy-start(bf16[8,16,6,16]{3,1,2,0:T(8,128)(2,1)} %copy.159) | copy-start | bytes 73732
  87.6 4.4 %copy-start.7 = (bf16[8,16,1152]{2,1,0:T(8,128)(2,1)S(1)}, bf16[8,16,1152]{2,1,0:T(8,128)(2,1)}, u32[]{:S(2)}) copy-start(bf16[8,16,1152]{2,1,0:T(8,128)(2,1)} %reshape.112) | copy-start | bytes 884740
  87.9 4.3 %copy-start.8 = (bf16[8,16,1152]{2,1,0:T(8,128)(2,1)S(1)}, bf16[8,16,1152]{2,1,0:T(8,128)(2,1)}, u32[]{:S(2)}) copy-start(bf16[8,16,1152]{2,1,0:T(8,128)(2,1)} %reshape.115) | copy-start | bytes 884740
  88.1 4.4 %copy-start.9 = (bf16[8,16,1152]{2,1,0:T(8,128)(2,1)S(1)}, bf16[8,16,1152]{2,1,0:T(8,128)(2,1)}, u32[]{:S(2)}) copy-start(bf16[8,16,1152]{2,1,0:T(8,128)(2,1)} %reshape.116) | copy-start | bytes 884740
  89.3 3.4 %copy-start.10 = (bf16[8,16,1152]{2,1,0:T(8,128)(2,1)S(1)}, bf16[8,16,1152]{2,1,0:T(8,128)(2,1)}, u32[]{:S(2)}) copy-start(bf16[8,16,1152]{2,1,0:T(8,128)(2,1)} %reshape.117) | copy-start | bytes 884740
  89.3 3.7 %copy-start.1 = (bf16[128,1152]{1,0:T(8,128)(2,1)S(1)}, bf16[128,1152]{1,0:T(8,128)(2,1)}, u32[]{:S(2)}) copy-start(bf16[128,1152]{1,0:T(8,128)(2,1)} %param.6) | copy-start | bytes 884740
  89.3 3.7 %copy-start.14 = (pred[8,16,1152]{2,1,0:T(8,128)(4,1)S(1)}, pred[8,16,1152]{2,1,0:T(8,128)(4,1)}, u32[]{:S(2)}) copy-start(pred[8,16,1152]{2,1,0:T(8,128)(4,1)} %broadcast_in_dim.45) | copy-start | bytes 442372
  92.5 1.5 %copy-start.11 = (bf16[8,16,1152]{2,1,0:T(8,128)(2,1)S(1)}, bf16[8,16,1152]{2,1,0:T(8,128)(2,1)}, u32[]{:S(2)}) copy-start(bf16[8,16,1152]{2,1,0:T(8,128)(2,1)} %reshape.123) | copy-start | bytes 884740
where the time goes:
time: 150 us; the launch traced here: 148 us
  local copies, waits for them, and re-layouts  62.8 us (42%)
  blocking collectives  52 us (35%)
  starting transfers between devices  18.6 us (12%)
  matrix products  7.35 us (5%)
  other arithmetic  6.23 us (4%)
    psum x1, blocking collectives, on_device(): summed = lax.psum(partial_sum, 'aux')  52 us
    slice x9, local copies, waits for them, and re-layouts, on_device(): density_ext[slot:slot + atom_count]  13 us
    ppermute x2, starting transfers between devices, extended(): after = lax.ppermute(first, axis, down)  12.8 us
    unnamed x58, local copies, waits for them, and re-layouts  9.19 us
    reshape x9, local copies, waits for them, and re-layouts, on_device(): shifted = shifted.reshape(atom_count, BS, local_funcs * band_width)  7.69 us
    reshape x2, local copies, waits for them, and re-layouts, on_device(): jnp.stack(pieces, axis=1).reshape(atom_count, band_width, band_width)  5.88 us
    ppermute x2, starting transfers between devices, extended(): before = lax.ppermute(last, axis, up)  5.86 us
    dot_general x9, matrix products, on_device(): jnp.einsum('ark,akn->arn', left_rows, spread_slot, preferred_element_type...  5.12 us
  transfers between devices with their start and end apart: 4, of which 0 were waited for; matrix products, arithmetic and copies ran while one was open for 45% of the time, Pallas kernels for 0%

commit v1 on v0

v1 whole, which is shorter than its diff:
```python
import jax
import jax.numpy as jnp
from jax import lax
from jax.experimental import pallas as pl
from jax.experimental.pallas import tpu as pltpu
from jax.sharding import PartitionSpec as P

BS = 16
HALF = 4
SLOTS = 2 * HALF + 1
WIDTH = SLOTS * BS
ATOMS = 8
ROWS = ATOMS * BS
SIDE = HALF * BS
WINDOW = (ATOMS + 2 * HALF) * BS
LANES = 128
VMEM = pl.BlockSpec(memory_space=pltpu.VMEM)
SMEM = pl.BlockSpec(memory_space=pltpu.SMEM)


def iota(shape, dim):
    return lax.broadcasted_iota(jnp.int32, shape, dim)


def window_sizes(size_ref):
    total = size_ref.shape[0]
    first = lax.axis_index("orb") * ATOMS + total - HALF
    return [size_ref[lax.rem(first + c, total)] for c in range(ATOMS + 2 * HALF)]


def kept_rows(pattern_ref, sizes):
    shape = (ATOMS, 2 * LANES)
    atom, lane = iota(shape, 0), iota(shape, 1)
    slot, func = lane // BS, lane % BS
    pattern = pattern_ref[...]
    live = jnp.zeros(shape, jnp.int32)
    for c, size in enumerate(sizes):
        live = jnp.where(atom + slot == c, size, live)
    on = jnp.zeros(shape, jnp.int32)
    for k in range(SLOTS):
        on = jnp.where(slot == k, pattern[:, k : k + 1], on)
    cols = jnp.where((func < live) & (on > 0), 1.0, 0.0)
    blocks = []
    for a in range(ATOMS):
        row = iota((BS, 2 * LANES), 0)
        block = jnp.broadcast_to(cols[a : a + 1], (BS, 2 * LANES))
        blocks.append(jnp.where(row < sizes[a + HALF], block, 0.0))
    return blocks


def moved(tile, shift):
    shift = shift % tile.shape[1]
    return tile if shift == 0 else pltpu.roll(tile, shift, 1)


def banded(ref, rows, start, shift, count):
    base = start - shift
    low = base // LANES
    off = base - low * LANES
    last = ref.shape[1] // LANES
    need = count + (1 if off else 0)
    tiles = []
    for i in range(low, low + need):
        i = min(max(i, 0), last - 1)
        tiles.append(ref[rows, i * LANES : (i + 1) * LANES])
    if not off:
        return jnp.concatenate(tiles, axis=1) if count > 1 else tiles[0]
    rolled = [pltpu.roll(t, LANES - off, 1) for t in tiles]
    lane = iota((BS, LANES), 1)
    out = [jnp.where(lane < LANES - off, rolled[i], rolled[i + 1]) for i in range(count)]
    return jnp.concatenate(out, axis=1) if count > 1 else out[0]


def pack_kernel(metric_ref, density_ref, pattern_ref, size_ref, up_ref, down_ref):
    sizes = window_sizes(size_ref)
    kept = kept_rows(pattern_ref, sizes)
    funcs = metric_ref.shape[1] // WIDTH
    for a in range(ATOMS):
        rows = slice(a * BS, (a + 1) * BS)
        if a < HALF:
            out_ref, out_rows = down_ref, slice(a * BS, (a + 1) * BS)
            shift = (2 * HALF + ATOMS - HALF + a - HALF) * BS - LANES
        else:
            out_ref, out_rows = up_ref, slice((a - HALF) * BS, (a - HALF + 1) * BS)
            shift = (a - ATOMS) * BS
        lane = iota((BS, 2 * LANES), 1)
        mask = moved(jnp.where(lane < WIDTH, kept[a], 0.0), shift)[:, :LANES]
        col = iota((BS, LANES), 1)
        inside = (col >= shift) & (col < shift + WIDTH)
        mask = jnp.where(inside, mask, 0.0).astype(jnp.bfloat16)
        for p in range(funcs):
            tile = banded(metric_ref, rows, p * WIDTH, shift, 1)
            out_ref[out_rows, p * LANES : (p + 1) * LANES] = tile * mask
        padded = jnp.concatenate(
            [density_ref[rows, :], jnp.zeros((BS, 2 * LANES - WIDTH), jnp.bfloat16)], axis=1
        )
        tile = moved(padded, shift)[:, :LANES]
        out_ref[out_rows, funcs * LANES : (funcs + 1) * LANES] = tile * mask


def main_kernel(
    three_ref,
    metric_ref,
    density_ref,
    pattern_ref,
    size_ref,
    before_ref,
    after_ref,
    out_ref,
    three_win,
    metric_win,
    density_win,
):
    sizes = window_sizes(size_ref)
    kept = kept_rows(pattern_ref, sizes)
    funcs = metric_ref.shape[1] // WIDTH
    lane = iota((BS, 2 * LANES), 1)
    kept = [jnp.where(lane < WIDTH, block, 0.0) for block in kept]
    zero_side = jnp.zeros((SIDE, LANES), jnp.bfloat16)
    density_win[0:SIDE, 0:LANES] = before_ref[:, funcs * LANES : (funcs + 1) * LANES]
    density_win[0:SIDE, LANES:] = zero_side
    density_win[SIDE + ROWS :, 0:LANES] = zero_side
    density_win[SIDE + ROWS :, LANES:] = after_ref[:, funcs * LANES : (funcs + 1) * LANES]
    for a in range(ATOMS):
        rows = slice(a * BS, (a + 1) * BS)
        mask = moved(kept[a], a * BS).astype(jnp.bfloat16)
        padded = jnp.concatenate(
            [density_ref[rows, :], jnp.zeros((BS, 2 * LANES - WIDTH), jnp.bfloat16)], axis=1
        )
        density_win[SIDE + a * BS : SIDE + (a + 1) * BS, :] = moved(padded, a * BS) * mask
        for p in range(funcs):
            three_win[p, rows, :] = banded(three_ref, rows, p * WIDTH, a * BS, 2) * mask
            metric_win[p, rows, :] = banded(metric_ref, rows, p * WIDTH, a * BS, 2) * mask
    atom = iota((ROWS, WINDOW), 0) // BS
    slot = iota((ROWS, WINDOW), 1) // BS - atom
    in_band = (slot >= 0) & (slot < SLOTS)
    density_all = density_win[...]
    contract_cols = (((1,), (1,)), ((), ()))
    own = jnp.zeros((ROWS, ROWS), jnp.float32)
    left = jnp.zeros((ROWS, SIDE), jnp.float32)
    right = jnp.zeros((ROWS, SIDE), jnp.float32)
    for p in range(funcs):
        spread = jnp.dot(three_win[p], density_all, preferred_element_type=jnp.float32)
        contracted = jnp.where(in_band, spread, 0.0).astype(jnp.bfloat16)
        cols = slice(p * LANES, (p + 1) * LANES)
        own += lax.dot_general(
            contracted, metric_win[p], contract_cols, preferred_element_type=jnp.float32
        )
        left += lax.dot_general(
            contracted[:, :LANES],
            before_ref[:, cols],
            contract_cols,
            preferred_element_type=jnp.float32,
        )
        right += lax.dot_general(
            contracted[:, LANES:],
            after_ref[:, cols],
            contract_cols,
            preferred_element_type=jnp.float32,
        )
    total = jnp.concatenate([left, own, right], axis=1)
    for a in range(ATOMS):
        rows = slice(a * BS, (a + 1) * BS)
        block = moved(total[rows], -a * BS) * kept[a]
        for h in range(2):
            out_ref[2 * a + h] = block[h * 8 : (h + 1) * 8, :WIDTH]


def on_device(three_center, metric_tensor, density, pattern, block_size):
    funcs = three_center.shape[1] // WIDTH
    message = jax.ShapeDtypeStruct((SIDE, (funcs + 1) * LANES), jnp.bfloat16)
    up, down = pl.pallas_call(
        pack_kernel,
        out_shape=(message, message),
        in_specs=[VMEM, VMEM, VMEM, SMEM],
        out_specs=(VMEM, VMEM),
        name="pack_halo",
    )(metric_tensor, density, pattern, block_size)
    peers = lax.axis_size("orb")
    onward = [(i, (i + 1) % peers) for i in range(peers)]
    back = [(j, i) for i, j in onward]
    before = lax.ppermute(up, "orb", onward)
    after = lax.ppermute(down, "orb", back)
    partial_sum = pl.pallas_call(
        main_kernel,
        out_shape=jax.ShapeDtypeStruct((ROWS // 8, 8, WIDTH), jnp.float32),
        in_specs=[VMEM, VMEM, VMEM, VMEM, SMEM, VMEM, VMEM],
        out_specs=VMEM,
        scratch_shapes=[
            pltpu.VMEM((funcs, ROWS, WINDOW), jnp.bfloat16),
            pltpu.VMEM((funcs, ROWS, WINDOW), jnp.bfloat16),
            pltpu.VMEM((WINDOW, WINDOW), jnp.bfloat16),
        ],
        name="exchange_terms",
    )(three_center, metric_tensor, density, pattern, block_size, before, after)
    terms = lax.all_to_all(partial_sum, "aux", 0, 0)
    return jnp.sum(terms, axis=0).astype(jnp.bfloat16)


def solution(mesh):
    placed = (P("orb", "aux"), P("orb", "aux"), P("orb", None), P("orb", None), P())
    return jax.shard_map(
        on_device, mesh=mesh, in_specs=placed, out_specs=P(("orb", "aux"), None), check_vma=False
    )
```

time: 150 us -> 44 us (0.29)
  the two profiles are of different devices: /device:TPU:1 before, /device:TPU:31 now
where the time goes in v1:
time: 44 us; the launch traced here: 43.7 us
  blocking collectives  21.4 us (49%)
  waiting for transfers between devices  7.89 us (18%)
  starting transfers between devices  6.24 us (14%)
  Pallas kernels  5.43 us (12%)
  local copies, waits for them, and re-layouts  2.15 us (5%)
  other arithmetic  0.61 us (1%)
    all_to_all x1, blocking collectives, on_device(): terms = lax.all_to_all(partial_sum, 'aux', 0, 0)  21.4 us
    ppermute x1, waiting for transfers between devices, on_device(): after = lax.ppermute(down, 'orb', back)  7.01 us
    ppermute x1, starting transfers between devices, on_device(): before = lax.ppermute(up, 'orb', onward)  4.32 us
    pallas_call x1, Pallas kernels, on_device(): pl.pallas_call(main_kernel, out_shape=jax.ShapeDtypeStruct((ROWS // 8, 8,...  3.54 us
    unnamed x5, local copies, waits for them, and re-layouts  2.15 us
    ppermute x1, starting transfers between devices, on_device(): after = lax.ppermute(down, 'orb', back)  1.92 us
    pallas_call x1, Pallas kernels, on_device(): pl.pallas_call(pack_kernel, out_shape=(message, message), in_specs=[VMEM,...  1.9 us
    ppermute x1, waiting for transfers between devices, on_device(): before = lax.ppermute(up, 'orb', onward)  0.88 us
  transfers between devices with their start and end apart: 2, of which 2 were waited for; matrix products, arithmetic and copies ran while one was open for 0% of the time, Pallas kernels for 0%

profile of v1, /device:TPU:31, one launch (start us, length us, event | category | flops | bytes accessed | tf_op | source)
XLA Modules:
  0.0 43.7 jit_solution(5868215266201185922)
XLA Ops:
  0.0 1.5 %copy.7.density_ref = bf16[128,144]{1,0:T(8,128)(2,1)} copy(bf16[128,144]{0,1:T(8,128)(2,1)} %param.7) | data formatting | bytes 73728 | tf_op args[2]
  1.5 1.9 %pack_halo.1 = (bf16[64,1152]{1,0:T(8,128)(2,1)}, bf16[64,1152]{1,0:T(8,128)(2,1)}) custom-call(bf16[128,1152]{1,0:T(8,128)(2,1)} %metric_ref.3, bf16[128,144]{1,0:T(8,128)(2,1)} %copy.7.density_ref, s32[8,9]{1,0:T(8,128)} %pattern_ref.3, s32[256]{0:T(256)} %size_ref.3), custom_call_target="tpu_custom_call" | custom-call | tf_op jit(solution)/shard_map/pack_halo/pallas_call | solution.py:172
  3.4 4.3 %collective-permute-start = (bf16[64,1152]{1,0:T(8,128)(2,1)}, bf16[64,1152]{1,0:T(8,128)(2,1)S(1)}, u32[]{:S(2)}, u32[]{:S(2)}) collective-permute-start(bf16[64,1152]{1,0:T(8,128)(2,1)} %get-tuple-element.7), channel_id=1, source_target_pairs={{0,16},{16,32},{32,48},{48,64},{64,80},{80,96},{96,112},{112,128},... | collective-permute-start | bytes 442376 | tf_op jit(solution)/shard_map/ppermute | solution.py:182
  7.7 1.9 %collective-permute-start.1 = (bf16[64,1152]{1,0:T(8,128)(2,1)}, bf16[64,1152]{1,0:T(8,128)(2,1)S(1)}, u32[]{:S(2)}, u32[]{:S(2)}) collective-permute-start(bf16[64,1152]{1,0:T(8,128)(2,1)} %get-tuple-element.8), channel_id=1, source_target_pairs={{16,0},{32,16},{48,32},{64,48},{80,64},{96,80},{112,96},{128,112},... | collective-permute-start | bytes 442376 | tf_op jit(solution)/shard_map/ppermute | solution.py:183
  9.6 0.9 %collective-permute-done.before_ref = bf16[64,1152]{1,0:T(8,128)(2,1)S(1)} collective-permute-done((bf16[64,1152]{1,0:T(8,128)(2,1)}, bf16[64,1152]{1,0:T(8,128)(2,1)S(1)}, u32[]{:S(2)}, u32[]{:S(2)}) %collective-permute-start) | collective-permute-done | bytes 147488 | tf_op jit(solution)/shard_map/ppermute | solution.py:182
  10.5 0.0 copy-start
  10.5 7.0 %collective-permute-done.1.after_ref = bf16[64,1152]{1,0:T(8,128)(2,1)S(1)} collective-permute-done((bf16[64,1152]{1,0:T(8,128)(2,1)}, bf16[64,1152]{1,0:T(8,128)(2,1)S(1)}, u32[]{:S(2)}, u32[]{:S(2)}) %collective-permute-start.1) | collective-permute-done | bytes 147488 | tf_op jit(solution)/shard_map/ppermute | solution.py:183
  17.5 0.0 copy-done
  17.5 0.0 copy-start.1
  17.5 0.7 %copy-done.1 = bf16[64,1152]{1,0:T(8,128)(2,1)} copy-done((bf16[64,1152]{1,0:T(8,128)(2,1)}, bf16[64,1152]{1,0:T(8,128)(2,1)S(1)}, u32[]{:S(2)}) %copy-start.1) | copy-done | bytes 147480
  18.2 3.5 %exchange_terms.1 = f32[16,8,144]{2,1,0:T(8,128)} custom-call(bf16[128,1152]{1,0:T(8,128)(2,1)} %three_ref.1, bf16[128,1152]{1,0:T(8,128)(2,1)} %metric_ref.3, bf16[128,144]{1,0:T(8,128)(2,1)} %copy.7.density_ref, s32[8,9]{1,0:T(8,128)} %pattern_ref.3, s32[256]{0:T(256)} %size_ref.3, bf16[64,1152]{1,0:T(8,128)(2,1)} %copy-done, bf16[64,1152]{1,0:T(8,128)(2,1)} %copy-done.1), custom_call_target="tpu_custom_call" | custom-call | tf_op jit(solution)/shard_map/exchange_terms/pallas_call | solution.py:184
  21.7 21.4 %all_to_all.5 = f32[16,8,144]{2,1,0:T(8,128)S(1)} all-to-all(f32[16,8,144]{2,1,0:T(8,128)} %exchange_terms.1), channel_id=1, replica_groups=mesh['orb'=32,'aux'=16] {'aux'}, dimensions={0} | all-to-all | bytes 147456 | tf_op jit(solution)/shard_map/all_to_all | solution.py:196
  43.1 0.6 %reduce_sum.9 = bf16[8,144]{1,0:T(8,128)(2,1)} reduce(f32[16,8,144]{2,1,0:T(8,128)S(1)} %all_to_all.5, f32[]{:T(128)} %constant.0.clone.1), dimensions={0}, to_apply=%region_0.0 | reduce | flops 17280 | bytes 76036 | tf_op jit(solution)/shard_map/reduce_sum | solution.py:197
Async XLA Ops:
  3.4 7.1 %collective-permute-start = (bf16[64,1152]{1,0:T(8,128)(2,1)}, bf16[64,1152]{1,0:T(8,128)(2,1)S(1)}, u32[]{:S(2)}, u32[]{:S(2)}) collective-permute-start(bf16[64,1152]{1,0:T(8,128)(2,1)} %get-tuple-element.7), channel_id=1, source_target_pairs={{0,16},{16,32},{32,48},{48,64},{64,80},{80,96},{96,112},{112,128},... | collective-permute-start | bytes 442376 | tf_op jit(solution)/shard_map/ppermute | solution.py:182
  7.7 9.8 %collective-permute-start.1 = (bf16[64,1152]{1,0:T(8,128)(2,1)}, bf16[64,1152]{1,0:T(8,128)(2,1)S(1)}, u32[]{:S(2)}, u32[]{:S(2)}) collective-permute-start(bf16[64,1152]{1,0:T(8,128)(2,1)} %get-tuple-element.8), channel_id=1, source_target_pairs={{16,0},{32,16},{48,32},{64,48},{80,64},{96,80},{112,96},{128,112},... | collective-permute-start | bytes 442376 | tf_op jit(solution)/shard_map/ppermute | solution.py:183
  10.5 7.0 %copy-start = (bf16[64,1152]{1,0:T(8,128)(2,1)}, bf16[64,1152]{1,0:T(8,128)(2,1)S(1)}, u32[]{:S(2)}) copy-start(bf16[64,1152]{1,0:T(8,128)(2,1)S(1)} %collective-permute-done.before_ref) | copy-start | bytes 442372
  17.5 0.7 %copy-start.1 = (bf16[64,1152]{1,0:T(8,128)(2,1)}, bf16[64,1152]{1,0:T(8,128)(2,1)S(1)}, u32[]{:S(2)}) copy-start(bf16[64,1152]{1,0:T(8,128)(2,1)S(1)} %collective-permute-done.1.after_ref) | copy-start | bytes 442372

commit v2 on v0

v2 whole, which is shorter than its diff:
```python
import jax
import jax.numpy as jnp
from jax import lax
from jax.experimental import pallas as pl
from jax.experimental.pallas import tpu as pltpu
from jax.sharding import PartitionSpec as P

BS = 16
HALF = 4
SLOTS = 2 * HALF + 1
WIDTH = SLOTS * BS
ATOMS = 8
ROWS = ATOMS * BS
SIDE = HALF * BS
WINDOW = (ATOMS + 2 * HALF) * BS
LANES = 128
PER = LANES // BS
VMEM = pl.BlockSpec(memory_space=pltpu.VMEM)
SMEM = pl.BlockSpec(memory_space=pltpu.SMEM)
HBM = pl.BlockSpec(memory_space=pltpu.HBM)
GRANT = 8 * 1024 * 1024
NT = (((1,), (1,)), ((), ()))


def iota(shape, dim):
    return lax.broadcasted_iota(jnp.int32, shape, dim)


def window_sizes(size_ref):
    total = size_ref.shape[0]
    first = lax.axis_index("orb") * ATOMS + total - HALF
    return [size_ref[lax.rem(first + c, total)] for c in range(ATOMS + 2 * HALF)]


def by_group(values):
    group = iota((8, LANES), 1) // BS
    out = jnp.zeros((8, LANES), jnp.int32)
    for g, value in values.items():
        out = jnp.where(group == g, value, out)
    return out


def row_mask(pattern_ref, sizes, a, first):
    limit = by_group(
        {
            c - first: pattern_ref[a, c - a] * sizes[c]
            for c in range(first, first + PER)
            if 0 <= c - a < SLOTS
        }
    )
    func = iota((8, LANES), 1) % BS
    row = iota((8, LANES), 0)
    size = sizes[a + HALF]
    halves = [jnp.where((func < limit) & (row + 8 * h < size), 1.0, 0.0) for h in range(2)]
    return jnp.concatenate(halves, axis=0).astype(jnp.bfloat16)


def banded(ref, rows, start, shift, count):
    base = start - shift
    low = base // LANES
    off = base - low * LANES
    last = ref.shape[1] // LANES
    need = count + (1 if off else 0)
    tiles = []
    for i in range(low, low + need):
        i = min(max(i, 0), last - 1)
        tiles.append(ref[rows, i * LANES : (i + 1) * LANES])
    if off:
        rolled = [pltpu.roll(t, LANES - off, 1) for t in tiles]
        lane = iota((BS, LANES), 1)
        tiles = [jnp.where(lane < LANES - off, rolled[i], rolled[i + 1]) for i in range(count)]
    return tiles


def density_rows(spread_ref, pattern_ref, sizes, slot_of, c):
    group = iota((BS, LANES), 1) // BS
    tile = jnp.zeros((BS, LANES), jnp.bfloat16)
    limits = {}
    for j, k in slot_of.items():
        tile = jnp.where(group == j, spread_ref[k * BS : (k + 1) * BS, :], tile)
        limits[j] = pattern_ref[j, k] * sizes[c[j]]
    limit = by_group(limits)
    own = by_group({j: sizes[j + HALF] for j in slot_of})
    live = iota((8, LANES), 1) % BS < own
    row = iota((8, LANES), 0)
    halves = [jnp.where((row + 8 * h < limit) & live, 1.0, 0.0) for h in range(2)]
    return tile * jnp.concatenate(halves, axis=0).astype(jnp.bfloat16)


def pack_halo(metric_ref, spread_ref, pattern_ref, sizes, up_ref, down_ref):
    funcs = metric_ref.shape[1] // WIDTH
    last = slice(funcs * LANES, (funcs + 1) * LANES)
    for a in range(ATOMS):
        rows = slice(a * BS, (a + 1) * BS)
        first = 0 if a < HALF else ATOMS
        out_ref = down_ref if a < HALF else up_ref
        out_rows = slice((a % HALF) * BS, (a % HALF + 1) * BS)
        mask = row_mask(pattern_ref, sizes, a, first)
        for p in range(funcs):
            tile = banded(metric_ref, rows, p * WIDTH, (a - first) * BS, 1)[0]
            out_ref[out_rows, p * LANES : (p + 1) * LANES] = tile * mask
    lane = iota((BS, LANES), 1)
    for g in range(HALF):
        tiles = []
        for c in (g, g + HALF):
            slot_of, atom_of = {}, {}
            for j in range(ATOMS):
                at = c if j < HALF else c + ATOMS
                if 0 <= at - j < SLOTS:
                    slot_of[j], atom_of[j] = at - j, at
            tiles.append(density_rows(spread_ref, pattern_ref, sizes, slot_of, atom_of))
        near, far = tiles[0], pltpu.roll(tiles[1], LANES // 2, 1)
        rows = slice(g * BS, (g + 1) * BS)
        down_ref[rows, last] = jnp.where(lane < LANES // 2, near, far)
        up_ref[rows, last] = jnp.where(lane < LANES // 2, far, near)


def pack_kernel(
    metric_hbm,
    spread_hbm,
    pattern_hbm,
    size_hbm,
    odd_up_ref,
    even_up_ref,
    metric_ref,
    spread_ref,
    pattern_ref,
    size_ref,
    sems,
):
    pairs = (
        (size_hbm, size_ref),
        (pattern_hbm, pattern_ref),
        (spread_hbm, spread_ref),
        (metric_hbm, metric_ref),
    )
    copies = [pltpu.make_async_copy(src, dst, sems.at[i]) for i, (src, dst) in enumerate(pairs)]
    for copy in copies:
        copy.start()
    for copy in copies:
        copy.wait()
    sizes = window_sizes(size_ref)
    odd = lax.rem(lax.axis_index("orb"), 2) == 1

    @pl.when(odd)
    def _():
        pack_halo(metric_ref, spread_ref, pattern_ref, sizes, odd_up_ref, even_up_ref)

    @pl.when(jnp.logical_not(odd))
    def _():
        pack_halo(metric_ref, spread_ref, pattern_ref, sizes, even_up_ref, odd_up_ref)


def prepare_kernel(
    three_ref, metric_ref, spread_ref, pattern_ref, size_ref, three_win, metric_win, spread_win, kept_win
):
    sizes = window_sizes(size_ref)
    funcs = metric_ref.shape[1] // WIDTH
    for a in range(ATOMS):
        rows = slice(a * BS, (a + 1) * BS)
        masks = [row_mask(pattern_ref, sizes, a, h * PER) for h in range(2)]
        for h in range(2):
            kept_win[rows, h * LANES : (h + 1) * LANES] = masks[h]
        for p in range(funcs):
            tiles = banded(three_ref, rows, p * WIDTH, a * BS, 2)
            for h in range(2):
                three_win[p, rows, h * LANES : (h + 1) * LANES] = tiles[h] * masks[h]
            tiles = banded(metric_ref, rows, p * WIDTH, a * BS, 2)
            for h in range(2):
                cols = slice(p * WINDOW + h * LANES, p * WINDOW + (h + 1) * LANES)
                metric_win[rows, cols] = tiles[h] * masks[h]
    lane = iota((BS, LANES), 1)
    zero = jnp.zeros((BS, LANES), jnp.bfloat16)
    for c in range(ATOMS + 2 * HALF):
        slot_of = {j: c - j for j in range(ATOMS) if 0 <= c - j < SLOTS}
        tile = density_rows(spread_ref, pattern_ref, sizes, slot_of, {j: c for j in slot_of})
        tile = pltpu.roll(tile, LANES // 2, 1)
        rows = slice(c * BS, (c + 1) * BS)
        spread_win[rows, :LANES] = jnp.where(lane < LANES // 2, zero, tile)
        spread_win[rows, LANES:] = jnp.where(lane < LANES // 2, tile, zero)


def main_kernel(three_win, metric_win, spread_win, kept_win, even_up_ref, odd_up_ref, out_ref, spread_all):
    funcs = three_win.shape[0]
    last = slice(funcs * LANES, (funcs + 1) * LANES)
    low = iota((SIDE, LANES), 1) < LANES // 2
    odd = lax.rem(lax.axis_index("orb"), 2) == 1

    def before(cols):
        return jnp.where(odd, even_up_ref[:, cols], odd_up_ref[:, cols])

    def after(cols):
        return jnp.where(odd, odd_up_ref[:, cols], even_up_ref[:, cols])

    spread_all[...] = spread_win[...]
    for h in range(2):
        tile = before(last)
        tile = pltpu.roll(tile, LANES // 2, 1) if h == 0 else tile
        rows = slice(h * SIDE, (h + 1) * SIDE)
        spread_all[rows, :LANES] = jnp.where(low, tile, spread_win[rows, :LANES])
        tile = after(last)
        tile = pltpu.roll(tile, LANES // 2, 1) if h == 0 else tile
        rows = slice((h + 2) * SIDE, (h + 3) * SIDE)
        spread_all[rows, LANES:] = jnp.where(low, spread_win[rows, LANES:], tile)
    atom = iota((ROWS, WINDOW), 0) // BS
    slot = iota((ROWS, WINDOW), 1) // BS - atom
    in_band = (slot >= 0) & (slot < SLOTS)
    spread = lax.dot_general(
        three_win[...].reshape(funcs * ROWS, WINDOW), spread_all[...], NT, preferred_element_type=jnp.float32
    )
    contracted = [
        jnp.where(in_band, spread[p * ROWS : (p + 1) * ROWS], 0.0).astype(jnp.bfloat16) for p in range(funcs)
    ]
    own = lax.dot_general(
        jnp.concatenate(contracted, axis=1), metric_win[...], NT, preferred_element_type=jnp.float32
    )
    near = [jnp.concatenate([c[:SIDE, :LANES], c[SIDE:, LANES:]], axis=0) for c in contracted]
    cols = slice(0, funcs * LANES)
    sides = lax.dot_general(
        jnp.concatenate(near, axis=1),
        jnp.concatenate([before(cols), after(cols)], axis=0),
        NT,
        preferred_element_type=jnp.float32,
    )
    total = jnp.concatenate([sides[:, :SIDE], own, sides[:, SIDE:]], axis=1)
    total = jnp.where(kept_win[...] > 0, total, 0.0)
    for a in range(ATOMS):
        block = total[a * BS : (a + 1) * BS]
        block = pltpu.roll(block, WINDOW - a * BS, 1) if a else block
        for h in range(2):
            out_ref[2 * a + h] = block[h * 8 : (h + 1) * 8, :WIDTH]


def call(kernel, out_shape, in_specs, name, flops=0, moved=0, scratch_shapes=()):
    return pl.pallas_call(
        kernel,
        out_shape=out_shape,
        in_specs=in_specs,
        out_specs=(VMEM,) * len(out_shape) if isinstance(out_shape, tuple) else VMEM,
        scratch_shapes=scratch_shapes,
        compiler_params=pltpu.CompilerParams(vmem_limit_bytes=GRANT),
        cost_estimate=pl.CostEstimate(flops=flops, bytes_accessed=moved, transcendentals=0),
        name=name,
    )


def on_device(three_center, metric_tensor, density, pattern, block_size):
    funcs = three_center.shape[1] // WIDTH
    spread = density.T
    message = pltpu.VMEM((SIDE, (funcs + 1) * LANES), jnp.bfloat16)
    odd_up, even_up = call(
        pack_kernel,
        (message, message),
        [HBM] * 4,
        "pack_halo",
        0,
        1 << 20,
        [
            pltpu.VMEM(metric_tensor.shape, jnp.bfloat16),
            pltpu.VMEM(spread.shape, jnp.bfloat16),
            pltpu.SMEM(pattern.shape, jnp.int32),
            pltpu.SMEM(block_size.shape, jnp.int32),
            pltpu.SemaphoreType.DMA((4,)),
        ],
    )(*[pltpu.with_memory_space_constraint(x, pltpu.HBM) for x in (metric_tensor, spread, pattern, block_size)])
    peers = lax.axis_size("orb")
    odd_pairs = [(i, (i + 1) % peers if i % 2 else (i - 1) % peers) for i in range(peers)]
    even_pairs = [(i, i + 1 if i % 2 == 0 else i - 1) for i in range(peers)]
    from_odd_up = lax.ppermute(odd_up, "orb", odd_pairs)
    from_even_up = lax.ppermute(even_up, "orb", even_pairs)
    wide = jax.ShapeDtypeStruct((funcs, ROWS, WINDOW), jnp.bfloat16)
    prepared = call(
        prepare_kernel,
        (
            wide,
            jax.ShapeDtypeStruct((ROWS, funcs * WINDOW), jnp.bfloat16),
            jax.ShapeDtypeStruct((WINDOW, WINDOW), jnp.bfloat16),
            jax.ShapeDtypeStruct((ROWS, WINDOW), jnp.bfloat16),
        ),
        [VMEM, VMEM, VMEM, SMEM, SMEM],
        "window_layout",
        0,
        2 << 20,
    )(three_center, metric_tensor, spread, pattern, block_size)
    partial_sum = call(
        main_kernel,
        jax.ShapeDtypeStruct((ROWS // 8, 8, WIDTH), jnp.float32),
        [VMEM] * 6,
        "exchange_terms",
        1 << 28,
        2 << 20,
        [pltpu.VMEM((WINDOW, WINDOW), jnp.bfloat16)],
    )(*prepared, from_even_up, from_odd_up)
    terms = lax.all_to_all(partial_sum, "aux", 0, 0)
    return jnp.sum(terms, axis=0).astype(jnp.bfloat16)


def solution(mesh):
    placed = (P("orb", "aux"), P("orb", "aux"), P("orb", None), P("orb", None), P())
    return jax.shard_map(
        on_device, mesh=mesh, in_specs=placed, out_specs=P(("orb", "aux"), None), check_vma=False
    )
```

time: 150 us -> 37.7 us (0.25); the launches traced: 148 us -> 37.5 us
  local copies, waits for them, and re-layouts: 62.8 us -> 0.97 us
  blocking collectives: 52 us -> 21.6 us
  starting transfers between devices: 18.6 us -> 10.6 us
  matrix products: 7.35 us -> 0 us
  other arithmetic: 6.23 us -> 0.61 us
  Pallas kernels: 0 us -> 3.16 us
    psum x1 -> x0, blocking collectives: 52 us -> none  [on_device(): summed = lax.psum(partial_sum, 'aux')]
    slice x29 -> x0, local copies, waits for them, and re-layouts: 25.1 us -> none  [the longest x9 13 us: on_device(): density_ext[slot:slot + atom_count]]
    all_to_all x0 -> x1, blocking collectives: none -> 21.6 us  [on_device(): terms = lax.all_to_all(partial_sum, 'aux', 0, 0)]
    reshape x14 -> x0, local copies, waits for them, and re-layouts: 14.5 us -> none  [the longest x9 7.69 us: on_device(): shifted = shifted.reshape(atom_count, BS, local_funcs * band_width)]
    unnamed x58 -> x10, local copies, waits for them, and re-layouts: 9.19 us -> 0.97 us
    ppermute x4 -> x2, starting transfers between devices: 18.6 us -> 10.6 us  [the longest x1 6.63 us: on_device(): from_odd_up = lax.ppermute(odd_up, 'orb', odd_pairs)]
    dot_general x18 -> x0, matrix products: 7.35 us -> none  [the longest x9 5.12 us: on_device(): jnp.einsum('ark,akn->arn', left_rows, spread_slot, preferred_element_type...]
    convert_element_type x11 -> x0, local copies, waits for them, and re-layouts: 5.43 us -> none  [the longest x9 4.75 us: on_device(): shifted = jnp.einsum('ark,akn->arn', left_rows, spread_slot, preferred_el...]
  transfers between devices with their start and end apart: 4 -> 2, of which waited for: 0 -> 1; matrix products, arithmetic and copies ran while one was open for 45% -> 0% of each run, Pallas kernels for 0% -> 3%
where the time goes in v2:
time: 37.7 us; the launch traced here: 37.5 us
  blocking collectives  21.6 us (57%)
  starting transfers between devices  10.6 us (28%)
  Pallas kernels  3.16 us (8%)
  local copies, waits for them, and re-layouts  0.97 us (3%)
  other arithmetic  0.61 us (2%)
  waiting for transfers between devices  0.51 us (1%)
    all_to_all x1, blocking collectives, on_device(): terms = lax.all_to_all(partial_sum, 'aux', 0, 0)  21.6 us
    ppermute x1, starting transfers between devices, on_device(): from_odd_up = lax.ppermute(odd_up, 'orb', odd_pairs)  6.63 us
    ppermute x1, starting transfers between devices, on_device(): from_even_up = lax.ppermute(even_up, 'orb', even_pairs)  3.95 us
    pallas_call x1, Pallas kernels, on_device(): call(pack_kernel, (message, message), [HBM] * 4, 'pack_halo', 0, 1 << 20,...  1.26 us
    pallas_call x1, Pallas kernels, on_device(): call(prepare_kernel, (wide, jax.ShapeDtypeStruct((ROWS, funcs * WINDOW),...  1.05 us
    unnamed x10, local copies, waits for them, and re-layouts  0.97 us
    pallas_call x1, Pallas kernels, on_device(): call(main_kernel, jax.ShapeDtypeStruct((ROWS // 8, 8, WIDTH), jnp.float32...  0.86 us
  transfers between devices with their start and end apart: 2, of which 1 were waited for; matrix products, arithmetic and copies ran while one was open for 0% of the time, Pallas kernels for 3%

profile of v2, /device:TPU:1, one launch (start us, length us, event | category | flops | bytes accessed | tf_op | source)
XLA Modules:
  0.0 37.5 jit_solution(12150735729988985366)
XLA Ops:
  0.0 0.0 copy-start
  0.0 0.0 copy-start.2
  0.0 0.0 copy-start.3
  0.0 1.3 %pack_halo.1 = (bf16[64,1152]{1,0:T(8,128)(2,1)S(1)}, bf16[64,1152]{1,0:T(8,128)(2,1)S(1)}) custom-call(bf16[128,1152]{1,0:T(8,128)(2,1)} %metric_hbm.1, bf16[144,128]{1,0:T(8,128)(2,1)} %bitcast.1, s32[8,9]{1,0:T(8,128)} %pattern_hbm.1, s32[256]{0:T(256)} %size_hbm.1), custom_call_target="tpu_custom_call" | custom-call | bytes 1048576 | tf_op jit(solution)/shard_map/pack_halo/pallas_call | solution.py:251
  1.3 0.0 copy-start.4
  1.3 4.0 %collective-permute-start = (bf16[64,1152]{1,0:T(8,128)(2,1)S(1)}, bf16[64,1152]{1,0:T(8,128)(2,1)S(1)}, u32[]{:S(2)}, u32[]{:S(2)}) collective-permute-start(bf16[64,1152]{1,0:T(8,128)(2,1)S(1)} %get-tuple-element.15), channel_id=1, source_target_pairs={{0,16},{16,0},{32,48},{48,32},{64,80},{80,64},{96,112},{112,96},{1... | collective-permute-start | bytes 442376 | tf_op jit(solution)/shard_map/ppermute | solution.py:270
  5.2 6.6 %collective-permute-start.1 = (bf16[64,1152]{1,0:T(8,128)(2,1)S(1)}, bf16[64,1152]{1,0:T(8,128)(2,1)S(1)}, u32[]{:S(2)}, u32[]{:S(2)}) collective-permute-start(bf16[64,1152]{1,0:T(8,128)(2,1)S(1)} %get-tuple-element.16), channel_id=1, source_target_pairs={{0,496},{16,32},{32,16},{48,64},{64,48},{80,96},{96,80},{112,128},... | collective-permute-start | bytes 442376 | tf_op jit(solution)/shard_map/ppermute | solution.py:269
  11.9 0.0 copy-done
  11.9 0.0 copy-done.2
  11.9 0.0 copy-done.3
  11.9 0.0 copy-done.4
  11.9 0.0 copy-start.1
  11.9 1.0 %copy-done.1 = bf16[128,1152]{1,0:T(8,128)(2,1)S(1)} copy-done((bf16[128,1152]{1,0:T(8,128)(2,1)S(1)}, bf16[128,1152]{1,0:T(8,128)(2,1)}, u32[]{:S(2)}) %copy-start.1) | copy-done | bytes 294936
  12.9 1.1 %window_layout.1 = (bf16[8,128,256]{2,1,0:T(8,128)(2,1)S(1)}, bf16[128,2048]{1,0:T(8,128)(2,1)S(1)}, bf16[256,256]{1,0:T(8,128)(2,1)S(1)}, bf16[128,256]{1,0:T(8,128)(2,1)S(1)}) custom-call(bf16[128,1152]{1,0:T(8,128)(2,1)S(1)} %copy-done.1, bf16[128,1152]{1,0:T(8,128)(2,1)S(1)} %copy-done, bf16[144,128]{1,0:T(8,128)(2,1)S(1)} %bitcast.2, ...), custom_call_target="tpu_custom_call" | custom-call | bytes 2097152 | tf_op jit(solution)/shard_map/window_layout/pallas_call | solution.py:272
  13.9 0.0 collective-permute-done.even_up_ref
  13.9 0.5 %collective-permute-done.1.odd_up_ref = bf16[64,1152]{1,0:T(8,128)(2,1)S(1)} collective-permute-done((bf16[64,1152]{1,0:T(8,128)(2,1)S(1)}, bf16[64,1152]{1,0:T(8,128)(2,1)S(1)}, u32[]{:S(2)}, u32[]{:S(2)}) %collective-permute-start.1) | collective-permute-done | bytes 147488 | tf_op jit(solution)/shard_map/ppermute | solution.py:269
  14.5 0.9 %exchange_terms.1 = f32[16,8,144]{2,1,0:T(8,128)S(1)} custom-call(bf16[8,128,256]{2,1,0:T(8,128)(2,1)S(1)} %get-tuple-element.11.three_win, bf16[128,2048]{1,0:T(8,128)(2,1)S(1)} %get-tuple-element.12.metric_win, bf16[256,256]{1,0:T(8,128)(2,1)S(1)} %get-tuple-element.13.spread_win, bf16[128,256]{1,0:T(8,128)(2,1)S(1)} %get-tuple-element.14.kept_win, ...), custom_call_target="tpu_custom_call" | custom-call | flops 268435456 | bytes 2097152 | tf_op jit(solution)/shard_map/exchange_terms/pallas_call | solution.py:285
  15.3 21.6 %all_to_all.5 = f32[16,8,144]{2,1,0:T(8,128)S(1)} all-to-all(f32[16,8,144]{2,1,0:T(8,128)S(1)} %exchange_terms.1), channel_id=1, replica_groups=mesh['orb'=32,'aux'=16] {'aux'}, dimensions={0} | all-to-all | bytes 147456 | tf_op jit(solution)/shard_map/all_to_all | solution.py:294
  36.9 0.6 %reduce_sum.9 = bf16[8,144]{1,0:T(8,128)(2,1)} reduce(f32[16,8,144]{2,1,0:T(8,128)S(1)} %all_to_all.5, f32[]{:T(128)} %constant.0.clone.1), dimensions={0}, to_apply=%region_0.0 | reduce | flops 17280 | bytes 76036 | tf_op jit(solution)/shard_map/reduce_sum | solution.py:295
Async XLA Ops:
  0.0 11.9 %copy-start = (bf16[128,1152]{1,0:T(8,128)(2,1)S(1)}, bf16[128,1152]{1,0:T(8,128)(2,1)}, u32[]{:S(2)}) copy-start(bf16[128,1152]{1,0:T(8,128)(2,1)} %metric_hbm.1) | copy-start | bytes 884740
  0.0 11.9 %copy-start.2 = (bf16[128,144]{0,1:T(8,128)(2,1)S(1)}, bf16[128,144]{0,1:T(8,128)(2,1)}, u32[]{:S(2)}) copy-start(bf16[128,144]{0,1:T(8,128)(2,1)} %param.7) | copy-start | bytes 110596
  0.0 11.9 %copy-start.3 = (s32[8,9]{1,0:T(8,128)S(1)}, s32[8,9]{1,0:T(8,128)}, u32[]{:S(2)}) copy-start(s32[8,9]{1,0:T(8,128)} %pattern_hbm.1) | copy-start | bytes 868
  1.3 10.6 %copy-start.4 = (s32[256]{0:T(256)S(1)}, s32[256]{0:T(256)}, u32[]{:S(2)}) copy-start(s32[256]{0:T(256)} %size_hbm.1) | copy-start | bytes 3076
  1.3 12.7 %collective-permute-start = (bf16[64,1152]{1,0:T(8,128)(2,1)S(1)}, bf16[64,1152]{1,0:T(8,128)(2,1)S(1)}, u32[]{:S(2)}, u32[]{:S(2)}) collective-permute-start(bf16[64,1152]{1,0:T(8,128)(2,1)S(1)} %get-tuple-element.15), channel_id=1, source_target_pairs={{0,16},{16,0},{32,48},{48,32},{64,80},{80,64},{96,112},{112,96},{1... | collective-permute-start | bytes 442376 | tf_op jit(solution)/shard_map/ppermute | solution.py:270
  5.2 9.2 %collective-permute-start.1 = (bf16[64,1152]{1,0:T(8,128)(2,1)S(1)}, bf16[64,1152]{1,0:T(8,128)(2,1)S(1)}, u32[]{:S(2)}, u32[]{:S(2)}) collective-permute-start(bf16[64,1152]{1,0:T(8,128)(2,1)S(1)} %get-tuple-element.16), channel_id=1, source_target_pairs={{0,496},{16,32},{32,16},{48,64},{64,48},{80,96},{96,80},{112,128},... | collective-permute-start | bytes 442376 | tf_op jit(solution)/shard_map/ppermute | solution.py:269
  11.9 1.0 %copy-start.1 = (bf16[128,1152]{1,0:T(8,128)(2,1)S(1)}, bf16[128,1152]{1,0:T(8,128)(2,1)}, u32[]{:S(2)}) copy-start(bf16[128,1152]{1,0:T(8,128)(2,1)} %three_ref.1) | copy-start | bytes 884740

commit v3 on v2

--- a/solution.py
+++ b/solution.py
@@ -228,7 +228,7 @@
         block = total[a * BS : (a + 1) * BS]
         block = pltpu.roll(block, WINDOW - a * BS, 1) if a else block
         for h in range(2):
-            out_ref[2 * a + h] = block[h * 8 : (h + 1) * 8, :WIDTH]
+            out_ref[2 * a + h] = block[h * 8 : (h + 1) * 8, :WIDTH].astype(jnp.bfloat16)
 
 
 def call(kernel, out_shape, in_specs, name, flops=0, moved=0, scratch_shapes=()):
@@ -284,7 +284,7 @@
     )(three_center, metric_tensor, spread, pattern, block_size)
     partial_sum = call(
         main_kernel,
-        jax.ShapeDtypeStruct((ROWS // 8, 8, WIDTH), jnp.float32),
+        jax.ShapeDtypeStruct((ROWS // 8, 8, WIDTH), jnp.bfloat16),
         [VMEM] * 6,
         "exchange_terms",
         1 << 28,
@@ -292,7 +292,7 @@
         [pltpu.VMEM((WINDOW, WINDOW), jnp.bfloat16)],
     )(*prepared, from_even_up, from_odd_up)
     terms = lax.all_to_all(partial_sum, "aux", 0, 0)
-    return jnp.sum(terms, axis=0).astype(jnp.bfloat16)
+    return jnp.sum(terms.astype(jnp.float32), axis=0).astype(jnp.bfloat16)
 
 
 def solution(mesh):

time: 37.7 us -> 36.4 us (0.966)
  blocking collectives: 21.6 us -> 20.2 us
    all_to_all x1, blocking collectives: 21.6 us -> 20.2 us  [on_device(): terms = lax.all_to_all(partial_sum, 'aux', 0, 0)]
where the time goes in v3:
time: 36.4 us; the launch traced here: 36.1 us
  blocking collectives  20.2 us (55%)
  starting transfers between devices  10.6 us (29%)
  Pallas kernels  3.17 us (9%)
  local copies, waits for them, and re-layouts  0.97 us (3%)
  other arithmetic  0.61 us (2%)
  waiting for transfers between devices  0.51 us (1%)
    all_to_all x1, blocking collectives, on_device(): terms = lax.all_to_all(partial_sum, 'aux', 0, 0)  20.2 us
    ppermute x1, starting transfers between devices, on_device(): from_odd_up = lax.ppermute(odd_up, 'orb', odd_pairs)  6.63 us
    ppermute x1, starting transfers between devices, on_device(): from_even_up = lax.ppermute(even_up, 'orb', even_pairs)  3.95 us
    pallas_call x1, Pallas kernels, on_device(): call(pack_kernel, (message, message), [HBM] * 4, 'pack_halo', 0, 1 << 20,...  1.26 us
    pallas_call x1, Pallas kernels, on_device(): call(prepare_kernel, (wide, jax.ShapeDtypeStruct((ROWS, funcs * WINDOW),...  1.05 us
    unnamed x10, local copies, waits for them, and re-layouts  0.97 us
    pallas_call x1, Pallas kernels, on_device(): call(main_kernel, jax.ShapeDtypeStruct((ROWS // 8, 8, WIDTH), jnp.bfloat1...  0.86 us
  transfers between devices with their start and end apart: 2, of which 1 were waited for; matrix products, arithmetic and copies ran while one was open for 0% of the time, Pallas kernels for 3%

profile of v3, /device:TPU:1, one launch (start us, length us, event | category | flops | bytes accessed | tf_op | source)
XLA Modules:
  0.0 36.1 jit_solution(18296378095940366412)
XLA Ops:
  0.0 0.0 copy-start
  0.0 0.0 copy-start.2
  0.0 0.0 copy-start.3
  0.0 1.3 %pack_halo.1 = (bf16[64,1152]{1,0:T(8,128)(2,1)S(1)}, bf16[64,1152]{1,0:T(8,128)(2,1)S(1)}) custom-call(bf16[128,1152]{1,0:T(8,128)(2,1)} %metric_hbm.1, bf16[144,128]{1,0:T(8,128)(2,1)} %bitcast.1, s32[8,9]{1,0:T(8,128)} %pattern_hbm.1, s32[256]{0:T(256)} %size_hbm.1), custom_call_target="tpu_custom_call" | custom-call | bytes 1048576 | tf_op jit(solution)/shard_map/pack_halo/pallas_call | solution.py:251
  1.3 0.0 copy-start.4
  1.3 4.0 %collective-permute-start = (bf16[64,1152]{1,0:T(8,128)(2,1)S(1)}, bf16[64,1152]{1,0:T(8,128)(2,1)S(1)}, u32[]{:S(2)}, u32[]{:S(2)}) collective-permute-start(bf16[64,1152]{1,0:T(8,128)(2,1)S(1)} %get-tuple-element.15), channel_id=1, source_target_pairs={{0,16},{16,0},{32,48},{48,32},{64,80},{80,64},{96,112},{112,96},{1... | collective-permute-start | bytes 442376 | tf_op jit(solution)/shard_map/ppermute | solution.py:270
  5.2 6.6 %collective-permute-start.1 = (bf16[64,1152]{1,0:T(8,128)(2,1)S(1)}, bf16[64,1152]{1,0:T(8,128)(2,1)S(1)}, u32[]{:S(2)}, u32[]{:S(2)}) collective-permute-start(bf16[64,1152]{1,0:T(8,128)(2,1)S(1)} %get-tuple-element.16), channel_id=1, source_target_pairs={{0,496},{16,32},{32,16},{48,64},{64,48},{80,96},{96,80},{112,128},... | collective-permute-start | bytes 442376 | tf_op jit(solution)/shard_map/ppermute | solution.py:269
  11.9 0.0 copy-done
  11.9 0.0 copy-done.2
  11.9 0.0 copy-done.3
  11.9 0.0 copy-done.4
  11.9 0.0 copy-start.1
  11.9 1.0 %copy-done.1 = bf16[128,1152]{1,0:T(8,128)(2,1)S(1)} copy-done((bf16[128,1152]{1,0:T(8,128)(2,1)S(1)}, bf16[128,1152]{1,0:T(8,128)(2,1)}, u32[]{:S(2)}) %copy-start.1) | copy-done | bytes 294936
  12.9 1.1 %window_layout.1 = (bf16[8,128,256]{2,1,0:T(8,128)(2,1)S(1)}, bf16[128,2048]{1,0:T(8,128)(2,1)S(1)}, bf16[256,256]{1,0:T(8,128)(2,1)S(1)}, bf16[128,256]{1,0:T(8,128)(2,1)S(1)}) custom-call(bf16[128,1152]{1,0:T(8,128)(2,1)S(1)} %copy-done.1, bf16[128,1152]{1,0:T(8,128)(2,1)S(1)} %copy-done, bf16[144,128]{1,0:T(8,128)(2,1)S(1)} %bitcast.2, ...), custom_call_target="tpu_custom_call" | custom-call | bytes 2097152 | tf_op jit(solution)/shard_map/window_layout/pallas_call | solution.py:272
  13.9 0.0 collective-permute-done.even_up_ref
  13.9 0.5 %collective-permute-done.1.odd_up_ref = bf16[64,1152]{1,0:T(8,128)(2,1)S(1)} collective-permute-done((bf16[64,1152]{1,0:T(8,128)(2,1)S(1)}, bf16[64,1152]{1,0:T(8,128)(2,1)S(1)}, u32[]{:S(2)}, u32[]{:S(2)}) %collective-permute-start.1) | collective-permute-done | bytes 147488 | tf_op jit(solution)/shard_map/ppermute | solution.py:269
  14.5 0.9 %exchange_terms.1 = bf16[16,8,144]{2,1,0:T(8,128)(2,1)S(1)} custom-call(bf16[8,128,256]{2,1,0:T(8,128)(2,1)S(1)} %get-tuple-element.11.three_win, bf16[128,2048]{1,0:T(8,128)(2,1)S(1)} %get-tuple-element.12.metric_win, bf16[256,256]{1,0:T(8,128)(2,1)S(1)} %get-tuple-element.13.spread_win, bf16[128,256]{1,0:T(8,128)(2,1)S(1)} %get-tuple-element.14.kept_win, ...), custom_call_target="tpu_custom_call" | custom-call | flops 268435456 | bytes 2097152 | tf_op jit(solution)/shard_map/exchange_terms/pallas_call | solution.py:285
  15.3 20.2 %all_to_all.5 = bf16[16,8,144]{2,1,0:T(8,128)(2,1)S(1)} all-to-all(bf16[16,8,144]{2,1,0:T(8,128)(2,1)S(1)} %exchange_terms.1), channel_id=1, replica_groups=mesh['orb'=32,'aux'=16] {'aux'}, dimensions={0} | all-to-all | bytes 73728 | tf_op jit(solution)/shard_map/all_to_all | solution.py:294
  35.5 0.6 %reduce_sum.12 = bf16[8,144]{1,0:T(8,128)(2,1)} reduce(bf16[16,8,144]{2,1,0:T(8,128)(2,1)S(1)} %all_to_all.5, bf16[]{:T(256)} %constant.2.clone.1), dimensions={0}, to_apply=%region_0.0 | reduce | flops 17280 | bytes 39170 | tf_op jit(solution)/shard_map/reduce_sum | solution.py:295
Async XLA Ops:
  0.0 11.9 %copy-start = (bf16[128,1152]{1,0:T(8,128)(2,1)S(1)}, bf16[128,1152]{1,0:T(8,128)(2,1)}, u32[]{:S(2)}) copy-start(bf16[128,1152]{1,0:T(8,128)(2,1)} %metric_hbm.1) | copy-start | bytes 884740
  0.0 11.9 %copy-start.2 = (bf16[128,144]{0,1:T(8,128)(2,1)S(1)}, bf16[128,144]{0,1:T(8,128)(2,1)}, u32[]{:S(2)}) copy-start(bf16[128,144]{0,1:T(8,128)(2,1)} %param.7) | copy-start | bytes 110596
  0.0 11.9 %copy-start.3 = (s32[8,9]{1,0:T(8,128)S(1)}, s32[8,9]{1,0:T(8,128)}, u32[]{:S(2)}) copy-start(s32[8,9]{1,0:T(8,128)} %pattern_hbm.1) | copy-start | bytes 868
  1.3 10.6 %copy-start.4 = (s32[256]{0:T(256)S(1)}, s32[256]{0:T(256)}, u32[]{:S(2)}) copy-start(s32[256]{0:T(256)} %size_hbm.1) | copy-start | bytes 3076
  1.3 12.7 %collective-permute-start = (bf16[64,1152]{1,0:T(8,128)(2,1)S(1)}, bf16[64,1152]{1,0:T(8,128)(2,1)S(1)}, u32[]{:S(2)}, u32[]{:S(2)}) collective-permute-start(bf16[64,1152]{1,0:T(8,128)(2,1)S(1)} %get-tuple-element.15), channel_id=1, source_target_pairs={{0,16},{16,0},{32,48},{48,32},{64,80},{80,64},{96,112},{112,96},{1... | collective-permute-start | bytes 442376 | tf_op jit(solution)/shard_map/ppermute | solution.py:270
  5.2 9.2 %collective-permute-start.1 = (bf16[64,1152]{1,0:T(8,128)(2,1)S(1)}, bf16[64,1152]{1,0:T(8,128)(2,1)S(1)}, u32[]{:S(2)}, u32[]{:S(2)}) collective-permute-start(bf16[64,1152]{1,0:T(8,128)(2,1)S(1)} %get-tuple-element.16), channel_id=1, source_target_pairs={{0,496},{16,32},{32,16},{48,64},{64,48},{80,96},{96,80},{112,128},... | collective-permute-start | bytes 442376 | tf_op jit(solution)/shard_map/ppermute | solution.py:269
  11.9 1.0 %copy-start.1 = (bf16[128,1152]{1,0:T(8,128)(2,1)S(1)}, bf16[128,1152]{1,0:T(8,128)(2,1)}, u32[]{:S(2)}) copy-start(bf16[128,1152]{1,0:T(8,128)(2,1)} %three_ref.1) | copy-start | bytes 884740

commit v4 on v3

--- a/solution.py
+++ b/solution.py
@@ -128,11 +128,12 @@
     size_ref,
     sems,
 ):
+    blocks = [pl.ds(a * BS, BS) for a in range(ATOMS)]
     pairs = (
         (size_hbm, size_ref),
         (pattern_hbm, pattern_ref),
         (spread_hbm, spread_ref),
-        (metric_hbm, metric_ref),
+        *((metric_hbm.at[rows], metric_ref.at[rows]) for rows in blocks),
     )
     copies = [pltpu.make_async_copy(src, dst, sems.at[i]) for i, (src, dst) in enumerate(pairs)]
     for copy in copies:
@@ -152,8 +153,19 @@
 
 
 def prepare_kernel(
-    three_ref, metric_ref, spread_ref, pattern_ref, size_ref, three_win, metric_win, spread_win, kept_win
+    three_ref,
+    metric_ref,
+    spread_ref,
+    pattern_ref,
+    size_ref,
+    message_ref,
+    three_win,
+    metric_win,
+    spread_win,
+    kept_win,
+    first_ref,
 ):
+    first_ref[...] = message_ref[...]
     sizes = window_sizes(size_ref)
     funcs = metric_ref.shape[1] // WIDTH
     for a in range(ATOMS):
@@ -180,17 +192,22 @@
         spread_win[rows, LANES:] = jnp.where(lane < LANES // 2, tile, zero)
 
 
-def main_kernel(three_win, metric_win, spread_win, kept_win, even_up_ref, odd_up_ref, out_ref, spread_all):
+def main_kernel(three_win, metric_win, spread_win, kept_win, first_ref, odd_up_ref, even_up_ref, out_ref, spread_all):
     funcs = three_win.shape[0]
     last = slice(funcs * LANES, (funcs + 1) * LANES)
     low = iota((SIDE, LANES), 1) < LANES // 2
     odd = lax.rem(lax.axis_index("orb"), 2) == 1
 
+    is_first = lax.axis_index("orb") == 0
+
+    def even(cols):
+        return jnp.where(is_first, first_ref[:, cols], even_up_ref[:, cols])
+
     def before(cols):
-        return jnp.where(odd, even_up_ref[:, cols], odd_up_ref[:, cols])
+        return jnp.where(odd, even(cols), odd_up_ref[:, cols])
 
     def after(cols):
-        return jnp.where(odd, odd_up_ref[:, cols], even_up_ref[:, cols])
+        return jnp.where(odd, odd_up_ref[:, cols], even(cols))
 
     spread_all[...] = spread_win[...]
     for h in range(2):
@@ -260,14 +277,16 @@
             pltpu.VMEM(spread.shape, jnp.bfloat16),
             pltpu.SMEM(pattern.shape, jnp.int32),
             pltpu.SMEM(block_size.shape, jnp.int32),
-            pltpu.SemaphoreType.DMA((4,)),
+            pltpu.SemaphoreType.DMA((3 + ATOMS,)),
         ],
     )(*[pltpu.with_memory_space_constraint(x, pltpu.HBM) for x in (metric_tensor, spread, pattern, block_size)])
     peers = lax.axis_size("orb")
     odd_pairs = [(i, (i + 1) % peers if i % 2 else (i - 1) % peers) for i in range(peers)]
     even_pairs = [(i, i + 1 if i % 2 == 0 else i - 1) for i in range(peers)]
+    ahead = (1, 0)
+    from_first_even = lax.ppermute(even_up, "orb", [ahead])
     from_odd_up = lax.ppermute(odd_up, "orb", odd_pairs)
-    from_even_up = lax.ppermute(even_up, "orb", even_pairs)
+    from_even_up = lax.ppermute(even_up, "orb", [pair for pair in even_pairs if pair != ahead])
     wide = jax.ShapeDtypeStruct((funcs, ROWS, WINDOW), jnp.bfloat16)
     prepared = call(
         prepare_kernel,
@@ -276,21 +295,22 @@
             jax.ShapeDtypeStruct((ROWS, funcs * WINDOW), jnp.bfloat16),
             jax.ShapeDtypeStruct((WINDOW, WINDOW), jnp.bfloat16),
             jax.ShapeDtypeStruct((ROWS, WINDOW), jnp.bfloat16),
+            message,
         ),
-        [VMEM, VMEM, VMEM, SMEM, SMEM],
+        [VMEM, VMEM, VMEM, SMEM, SMEM, VMEM],
         "window_layout",
         0,
         2 << 20,
-    )(three_center, metric_tensor, spread, pattern, block_size)
+    )(three_center, metric_tensor, spread, pattern, block_size, from_first_even)
     partial_sum = call(
         main_kernel,
         jax.ShapeDtypeStruct((ROWS // 8, 8, WIDTH), jnp.bfloat16),
-        [VMEM] * 6,
+        [VMEM] * 7,
         "exchange_terms",
         1 << 28,
         2 << 20,
         [pltpu.VMEM((WINDOW, WINDOW), jnp.bfloat16)],
-    )(*prepared, from_even_up, from_odd_up)
+    )(*prepared, from_odd_up, from_even_up)
     terms = lax.all_to_all(partial_sum, "aux", 0, 0)
     return jnp.sum(terms.astype(jnp.float32), axis=0).astype(jnp.bfloat16)
 

time: 36.4 us -> 35.2 us (0.967)
  starting transfers between devices: 10.6 us -> 10.1 us
  waiting for transfers between devices: 0.51 us -> 0.01 us
    ppermute x1 -> x2, starting transfers between devices: 3.95 us -> 2.59 us  [the longest x1 1.3 us: on_device(): lax.ppermute(even_up, 'orb', [pair for pair in even_pairs if pair != ahead])]
    ppermute x1, starting transfers between devices: 6.63 us -> 7.5 us  [on_device(): from_odd_up = lax.ppermute(odd_up, 'orb', odd_pairs)]
    ppermute x1, waiting for transfers between devices: 0.51 us -> 0.01 us  [on_device(): from_odd_up = lax.ppermute(odd_up, 'orb', odd_pairs)]
  transfers between devices with their start and end apart: 2 -> 3, of which waited for: 1 -> 0; matrix products, arithmetic and copies ran while one was open for 0% -> 0% of each run, Pallas kernels for 3% -> 3%
where the time goes in v4:
time: 35.2 us; the launch traced here: 34.8 us
  blocking collectives  19.9 us (57%)
  starting transfers between devices  10.1 us (29%)
  Pallas kernels  3.16 us (9%)
  local copies, waits for them, and re-layouts  0.97 us (3%)
  other arithmetic  0.61 us (2%)
    all_to_all x1, blocking collectives, on_device(): terms = lax.all_to_all(partial_sum, 'aux', 0, 0)  19.9 us
    ppermute x1, starting transfers between devices, on_device(): from_odd_up = lax.ppermute(odd_up, 'orb', odd_pairs)  7.5 us
    ppermute x1, starting transfers between devices, on_device(): lax.ppermute(even_up, 'orb', [pair for pair in even_pairs if pair != ahead])  1.3 us
    ppermute x1, starting transfers between devices, on_device(): from_first_even = lax.ppermute(even_up, 'orb', [ahead])  1.29 us
    pallas_call x1, Pallas kernels, on_device(): call(pack_kernel, (message, message), [HBM] * 4, 'pack_halo', 0, 1 << 20,...  1.24 us
    pallas_call x1, Pallas kernels, on_device(): call(prepare_kernel, (wide, jax.ShapeDtypeStruct((ROWS, funcs * WINDOW),...  1.05 us
    unnamed x10, local copies, waits for them, and re-layouts  0.97 us
    pallas_call x1, Pallas kernels, on_device(): call(main_kernel, jax.ShapeDtypeStruct((ROWS // 8, 8, WIDTH), jnp.bfloat1...  0.86 us
  transfers between devices with their start and end apart: 3, of which 0 were waited for; matrix products, arithmetic and copies ran while one was open for 0% of the time, Pallas kernels for 3%

profile of v4, /device:TPU:1, one launch (start us, length us, event | category | flops | bytes accessed | tf_op | source)
XLA Modules:
  0.0 34.8 jit_solution(14947052751699646232)
XLA Ops:
  0.0 0.0 copy-start
  0.0 0.0 copy-start.2
  0.0 0.0 copy-start.3
  0.0 1.2 %pack_halo.1 = (bf16[64,1152]{1,0:T(8,128)(2,1)S(1)}, bf16[64,1152]{1,0:T(8,128)(2,1)S(1)}) custom-call(bf16[128,1152]{1,0:T(8,128)(2,1)} %metric_ref.1, bf16[144,128]{1,0:T(8,128)(2,1)} %bitcast.1, s32[8,9]{1,0:T(8,128)} %pattern_ref.1, s32[256]{0:T(256)} %size_ref.1), custom_call_target="tpu_custom_call" | custom-call | bytes 1048576 | tf_op jit(solution)/shard_map/pack_halo/pallas_call | solution.py:268
  1.3 0.0 copy-start.4
  1.3 1.3 %collective-permute-start = (bf16[64,1152]{1,0:T(8,128)(2,1)S(1)}, bf16[64,1152]{1,0:T(8,128)(2,1)S(1)}, u32[]{:S(2)}, u32[]{:S(2)}) collective-permute-start(bf16[64,1152]{1,0:T(8,128)(2,1)S(1)} %get-tuple-element.12), channel_id=1, source_target_pairs={{16,0},{17,1},{18,2},{19,3},{20,4},{21,5},{22,6},{23,7},{24,8},{25... | collective-permute-start | bytes 442376 | tf_op jit(solution)/shard_map/ppermute | solution.py:287
  2.6 7.5 %collective-permute-start.1 = (bf16[64,1152]{1,0:T(8,128)(2,1)S(1)}, bf16[64,1152]{1,0:T(8,128)(2,1)S(1)}, u32[]{:S(2)}, u32[]{:S(2)}) collective-permute-start(bf16[64,1152]{1,0:T(8,128)(2,1)S(1)} %get-tuple-element.18), channel_id=1, source_target_pairs={{0,496},{16,32},{32,16},{48,64},{64,48},{80,96},{96,80},{112,128},... | collective-permute-start | bytes 442376 | tf_op jit(solution)/shard_map/ppermute | solution.py:288
  10.1 1.3 %collective-permute-start.2 = (bf16[64,1152]{1,0:T(8,128)(2,1)S(1)}, bf16[64,1152]{1,0:T(8,128)(2,1)S(1)}, u32[]{:S(2)}, u32[]{:S(2)}) collective-permute-start(bf16[64,1152]{1,0:T(8,128)(2,1)S(1)} %get-tuple-element.12), channel_id=1, source_target_pairs={{0,16},{32,48},{48,32},{64,80},{80,64},{96,112},{112,96},{128,144}... | collective-permute-start | bytes 442376 | tf_op jit(solution)/shard_map/ppermute | solution.py:289
  11.4 0.0 collective-permute-done.message_ref
  11.4 0.0 copy-done
  11.4 0.0 copy-done.2
  11.4 0.0 copy-done.3
  11.4 0.0 copy-done.4
  11.4 0.0 copy-start.1
  11.5 1.0 %copy-done.1 = bf16[128,1152]{1,0:T(8,128)(2,1)S(1)} copy-done((bf16[128,1152]{1,0:T(8,128)(2,1)S(1)}, bf16[128,1152]{1,0:T(8,128)(2,1)}, u32[]{:S(2)}) %copy-start.1) | copy-done | bytes 294936
  12.4 1.1 %window_layout.1 = (bf16[8,128,256]{2,1,0:T(8,128)(2,1)S(1)}, bf16[128,2048]{1,0:T(8,128)(2,1)S(1)}, bf16[256,256]{1,0:T(8,128)(2,1)S(1)}, bf16[128,256]{1,0:T(8,128)(2,1)S(1)}, bf16[64,1152]{1,0:T(8,128)(2,1)S(1)}) custom-call(bf16[128,1152]{1,0:T(8,128)(2,1)S(1)} %copy-done.1, bf16[128,1152]{1,0:T(8,128)(2,1)S(1)} %copy-done, ...), custom_call_target="tpu_custom_call" | custom-call | bytes 2097152 | tf_op jit(solution)/shard_map/window_layout/pallas_call | solution.py:291
  13.5 0.0 collective-permute-done.1.odd_up_ref
  13.5 0.0 collective-permute-done.2.even_up_ref
  13.5 0.9 %exchange_terms.1 = bf16[16,8,144]{2,1,0:T(8,128)(2,1)S(1)} custom-call(bf16[8,128,256]{2,1,0:T(8,128)(2,1)S(1)} %get-tuple-element.13.three_win, bf16[128,2048]{1,0:T(8,128)(2,1)S(1)} %get-tuple-element.14.metric_win, bf16[256,256]{1,0:T(8,128)(2,1)S(1)} %get-tuple-element.15.spread_win, bf16[128,256]{1,0:T(8,128)(2,1)S(1)} %get-tuple-element.16.kept_win, ...), custom_call_target="tpu_custom_call" | custom-call | flops 268435456 | bytes 2097152 | tf_op jit(solution)/shard_map/exchange_terms/pallas_call | solution.py:305
  14.3 19.9 %all_to_all.5 = bf16[16,8,144]{2,1,0:T(8,128)(2,1)S(1)} all-to-all(bf16[16,8,144]{2,1,0:T(8,128)(2,1)S(1)} %exchange_terms.1), channel_id=1, replica_groups=mesh['orb'=32,'aux'=16] {'aux'}, dimensions={0} | all-to-all | bytes 73728 | tf_op jit(solution)/shard_map/all_to_all | solution.py:314
  34.2 0.6 %reduce_sum.12 = bf16[8,144]{1,0:T(8,128)(2,1)} reduce(bf16[16,8,144]{2,1,0:T(8,128)(2,1)S(1)} %all_to_all.5, bf16[]{:T(256)} %constant.2.clone.1), dimensions={0}, to_apply=%region_0.0 | reduce | flops 17280 | bytes 39170 | tf_op jit(solution)/shard_map/reduce_sum | solution.py:315
Async XLA Ops:
  0.0 11.4 %copy-start = (bf16[128,1152]{1,0:T(8,128)(2,1)S(1)}, bf16[128,1152]{1,0:T(8,128)(2,1)}, u32[]{:S(2)}) copy-start(bf16[128,1152]{1,0:T(8,128)(2,1)} %metric_ref.1) | copy-start | bytes 884740
  0.0 11.4 %copy-start.2 = (bf16[128,144]{0,1:T(8,128)(2,1)S(1)}, bf16[128,144]{0,1:T(8,128)(2,1)}, u32[]{:S(2)}) copy-start(bf16[128,144]{0,1:T(8,128)(2,1)} %param.7) | copy-start | bytes 110596
  0.0 11.4 %copy-start.3 = (s32[8,9]{1,0:T(8,128)S(1)}, s32[8,9]{1,0:T(8,128)}, u32[]{:S(2)}) copy-start(s32[8,9]{1,0:T(8,128)} %pattern_ref.1) | copy-start | bytes 868
  1.3 10.2 %copy-start.4 = (s32[256]{0:T(256)S(1)}, s32[256]{0:T(256)}, u32[]{:S(2)}) copy-start(s32[256]{0:T(256)} %size_ref.1) | copy-start | bytes 3076
  1.3 10.1 %collective-permute-start = (bf16[64,1152]{1,0:T(8,128)(2,1)S(1)}, bf16[64,1152]{1,0:T(8,128)(2,1)S(1)}, u32[]{:S(2)}, u32[]{:S(2)}) collective-permute-start(bf16[64,1152]{1,0:T(8,128)(2,1)S(1)} %get-tuple-element.12), channel_id=1, source_target_pairs={{16,0},{17,1},{18,2},{19,3},{20,4},{21,5},{22,6},{23,7},{24,8},{25... | collective-permute-start | bytes 442376 | tf_op jit(solution)/shard_map/ppermute | solution.py:287
  2.6 10.9 %collective-permute-start.1 = (bf16[64,1152]{1,0:T(8,128)(2,1)S(1)}, bf16[64,1152]{1,0:T(8,128)(2,1)S(1)}, u32[]{:S(2)}, u32[]{:S(2)}) collective-permute-start(bf16[64,1152]{1,0:T(8,128)(2,1)S(1)} %get-tuple-element.18), channel_id=1, source_target_pairs={{0,496},{16,32},{32,16},{48,64},{64,48},{80,96},{96,80},{112,128},... | collective-permute-start | bytes 442376 | tf_op jit(solution)/shard_map/ppermute | solution.py:288
  10.1 3.4 %collective-permute-start.2 = (bf16[64,1152]{1,0:T(8,128)(2,1)S(1)}, bf16[64,1152]{1,0:T(8,128)(2,1)S(1)}, u32[]{:S(2)}, u32[]{:S(2)}) collective-permute-start(bf16[64,1152]{1,0:T(8,128)(2,1)S(1)} %get-tuple-element.12), channel_id=1, source_target_pairs={{0,16},{32,48},{48,32},{64,80},{80,64},{96,112},{112,96},{128,144}... | collective-permute-start | bytes 442376 | tf_op jit(solution)/shard_map/ppermute | solution.py:289
  11.4 1.0 %copy-start.1 = (bf16[128,1152]{1,0:T(8,128)(2,1)S(1)}, bf16[128,1152]{1,0:T(8,128)(2,1)}, u32[]{:S(2)}) copy-start(bf16[128,1152]{1,0:T(8,128)(2,1)} %three_ref.1) | copy-start | bytes 884740

commit v5 on v4

--- a/solution.py
+++ b/solution.py
@@ -1,3 +1,5 @@
+import functools
+
 import jax
 import jax.numpy as jnp
 from jax import lax
@@ -20,6 +22,7 @@
 HBM = pl.BlockSpec(memory_space=pltpu.HBM)
 GRANT = 8 * 1024 * 1024
 NT = (((1,), (1,)), ((), ()))
+AHEAD = (0, 20, 24, 28)
 
 
 def iota(shape, dim):
@@ -192,13 +195,16 @@
         spread_win[rows, LANES:] = jnp.where(lane < LANES // 2, tile, zero)
 
 
-def main_kernel(three_win, metric_win, spread_win, kept_win, first_ref, odd_up_ref, even_up_ref, out_ref, spread_all):
+def main_kernel(place, three_win, metric_win, spread_win, kept_win, first_ref, odd_up_ref, even_up_ref, out_ref, spread_all):
     funcs = three_win.shape[0]
     last = slice(funcs * LANES, (funcs + 1) * LANES)
     low = iota((SIDE, LANES), 1) < LANES // 2
     odd = lax.rem(lax.axis_index("orb"), 2) == 1
 
-    is_first = lax.axis_index("orb") == 0
+    here = lax.axis_index("orb")
+    is_first = lax.rem(lax.axis_index("aux"), 2) == 1
+    for target in AHEAD:
+        is_first |= here == target
 
     def even(cols):
         return jnp.where(is_first, first_ref[:, cols], even_up_ref[:, cols])
@@ -245,7 +251,7 @@
         block = total[a * BS : (a + 1) * BS]
         block = pltpu.roll(block, WINDOW - a * BS, 1) if a else block
         for h in range(2):
-            out_ref[2 * a + h] = block[h * 8 : (h + 1) * 8, :WIDTH].astype(jnp.bfloat16)
+            out_ref[place[2 * a + h]] = block[h * 8 : (h + 1) * 8, :WIDTH].astype(jnp.bfloat16)
 
 
 def call(kernel, out_shape, in_specs, name, flops=0, moved=0, scratch_shapes=()):
@@ -280,13 +286,21 @@
             pltpu.SemaphoreType.DMA((3 + ATOMS,)),
         ],
     )(*[pltpu.with_memory_space_constraint(x, pltpu.HBM) for x in (metric_tensor, spread, pattern, block_size)])
-    peers = lax.axis_size("orb")
+    peers, funcs_at = lax.axis_size("orb"), lax.axis_size("aux")
     odd_pairs = [(i, (i + 1) % peers if i % 2 else (i - 1) % peers) for i in range(peers)]
     even_pairs = [(i, i + 1 if i % 2 == 0 else i - 1) for i in range(peers)]
-    ahead = (1, 0)
-    from_first_even = lax.ppermute(even_up, "orb", [ahead])
-    from_odd_up = lax.ppermute(odd_up, "orb", odd_pairs)
-    from_even_up = lax.ppermute(even_up, "orb", [pair for pair in even_pairs if pair != ahead])
+    ahead = [(i + 1, i) for i in AHEAD]
+    behind = [pair for pair in even_pairs if pair not in ahead]
+
+    def swap(message, *pairs_of_core):
+        pairs = [
+            (i * funcs_at + z, j * funcs_at + z) for z in range(funcs_at) for i, j in pairs_of_core[z % 2]
+        ]
+        return lax.ppermute(message, ("orb", "aux"), pairs)
+
+    from_first_even = swap(even_up, ahead, even_pairs)
+    from_odd_up = swap(odd_up, odd_pairs, odd_pairs)
+    from_even_up = swap(even_up, behind, [])
     wide = jax.ShapeDtypeStruct((funcs, ROWS, WINDOW), jnp.bfloat16)
     prepared = call(
         prepare_kernel,
@@ -302,8 +316,10 @@
         0,
         2 << 20,
     )(three_center, metric_tensor, spread, pattern, block_size, from_first_even)
+    lead = funcs_at - 3
+    order = [lead] + [i for i in range(funcs_at) if i != lead]
     partial_sum = call(
-        main_kernel,
+        functools.partial(main_kernel, [order.index(i) for i in range(funcs_at)]),
         jax.ShapeDtypeStruct((ROWS // 8, 8, WIDTH), jnp.bfloat16),
         [VMEM] * 7,
         "exchange_terms",
@@ -311,7 +327,7 @@
         2 << 20,
         [pltpu.VMEM((WINDOW, WINDOW), jnp.bfloat16)],
     )(*prepared, from_odd_up, from_even_up)
-    terms = lax.all_to_all(partial_sum, "aux", 0, 0)
+    terms = lax.all_to_all(partial_sum, "aux", 0, 0, axis_index_groups=[order])
     return jnp.sum(terms.astype(jnp.float32), axis=0).astype(jnp.bfloat16)
 
 

time: 35.2 us -> 32.8 us (0.932)
  blocking collectives: 19.9 us -> 15.9 us
  starting transfers between devices: 10.1 us -> 11.2 us
  waiting for transfers between devices: 0.01 us -> 0.59 us
    all_to_all x1, blocking collectives: 19.9 us -> 15.9 us  [on_device(): terms = lax.all_to_all(partial_sum, 'aux', 0, 0, axis_index_groups=[order])]
    ppermute x3, starting transfers between devices: 10.1 us -> 11.2 us  [swap(): return lax.ppermute(message, ('orb', 'aux'), pairs)]
    ppermute x3, waiting for transfers between devices: 0.01 us -> 0.59 us  [swap(): return lax.ppermute(message, ('orb', 'aux'), pairs)]
  transfers between devices with their start and end apart: 3 -> 3, of which waited for: 0 -> 1; matrix products, arithmetic and copies ran while one was open for 0% -> 0% of each run, Pallas kernels for 3% -> 3%
where the time goes in v5:
time: 32.8 us; the launch traced here: 32.6 us
  blocking collectives  15.9 us (48%)
  starting transfers between devices  11.2 us (34%)
  Pallas kernels  3.16 us (10%)
  local copies, waits for them, and re-layouts  0.97 us (3%)
  other arithmetic  0.61 us (2%)
  waiting for transfers between devices  0.59 us (2%)
    all_to_all x1, blocking collectives, on_device(): terms = lax.all_to_all(partial_sum, 'aux', 0, 0, axis_index_groups=[order])  15.9 us
    ppermute x3, starting transfers between devices, swap(): return lax.ppermute(message, ('orb', 'aux'), pairs)  11.2 us
    pallas_call x1, Pallas kernels, on_device(): call(pack_kernel, (message, message), [HBM] * 4, 'pack_halo', 0, 1 << 20,...  1.24 us
    pallas_call x1, Pallas kernels, on_device(): call(prepare_kernel, (wide, jax.ShapeDtypeStruct((ROWS, funcs * WINDOW),...  1.05 us
    unnamed x10, local copies, waits for them, and re-layouts  0.97 us
    pallas_call x1, Pallas kernels, on_device(): call(functools.partial(main_kernel, [order.index(i) for i in range(funcs_...  0.86 us
  transfers between devices with their start and end apart: 3, of which 1 were waited for; matrix products, arithmetic and copies ran while one was open for 0% of the time, Pallas kernels for 3%

profile of v5, /device:TPU:1, one launch (start us, length us, event | category | flops | bytes accessed | tf_op | source)
XLA Modules:
  0.0 32.6 jit_solution(540351508730638888)
XLA Ops:
  0.0 0.0 copy-start
  0.0 0.0 copy-start.2
  0.0 0.0 copy-start.3
  0.0 1.2 %pack_halo.1 = (bf16[64,1152]{1,0:T(8,128)(2,1)S(1)}, bf16[64,1152]{1,0:T(8,128)(2,1)S(1)}) custom-call(bf16[128,1152]{1,0:T(8,128)(2,1)} %metric_ref.1, bf16[144,128]{1,0:T(8,128)(2,1)} %bitcast.1, s32[8,9]{1,0:T(8,128)} %pattern_ref.1, s32[256]{0:T(256)} %size_ref.1), custom_call_target="tpu_custom_call" | custom-call | bytes 1048576 | tf_op jit(solution)/shard_map/pack_halo/pallas_call | solution.py:274
  1.3 0.0 copy-start.4
  1.3 4.0 %collective-permute-start = (bf16[64,1152]{1,0:T(8,128)(2,1)S(1)}, bf16[64,1152]{1,0:T(8,128)(2,1)S(1)}, u32[]{:S(2)}, u32[]{:S(2)}) collective-permute-start(bf16[64,1152]{1,0:T(8,128)(2,1)S(1)} %get-tuple-element.12), channel_id=1, source_target_pairs={{16,0},{336,320},{400,384},{464,448},{1,17},{17,1},{33,49},{49,33}... | collective-permute-start | bytes 442376 | tf_op jit(solution)/shard_map/ppermute | solution.py:299
  5.2 6.6 %collective-permute-start.1 = (bf16[64,1152]{1,0:T(8,128)(2,1)S(1)}, bf16[64,1152]{1,0:T(8,128)(2,1)S(1)}, u32[]{:S(2)}, u32[]{:S(2)}) collective-permute-start(bf16[64,1152]{1,0:T(8,128)(2,1)S(1)} %get-tuple-element.18), channel_id=1, source_target_pairs={{0,496},{16,32},{32,16},{48,64},{64,48},{80,96},{96,80},{112,128},... | collective-permute-start | bytes 442376 | tf_op jit(solution)/shard_map/ppermute | solution.py:299
  11.9 0.7 %collective-permute-start.2 = (bf16[64,1152]{1,0:T(8,128)(2,1)S(1)}, bf16[64,1152]{1,0:T(8,128)(2,1)S(1)}, u32[]{:S(2)}, u32[]{:S(2)}) collective-permute-start(bf16[64,1152]{1,0:T(8,128)(2,1)S(1)} %get-tuple-element.12), channel_id=1, source_target_pairs={{0,16},{32,48},{48,32},{64,80},{80,64},{96,112},{112,96},{128,144}... | collective-permute-start | bytes 442376 | tf_op jit(solution)/shard_map/ppermute | solution.py:299
  12.5 0.0 collective-permute-done.message_ref
  12.6 0.0 copy-done
  12.6 0.0 copy-done.2
  12.6 0.0 copy-done.3
  12.6 0.0 copy-done.4
  12.6 0.0 copy-start.1
  12.6 1.0 %copy-done.1 = bf16[128,1152]{1,0:T(8,128)(2,1)S(1)} copy-done((bf16[128,1152]{1,0:T(8,128)(2,1)S(1)}, bf16[128,1152]{1,0:T(8,128)(2,1)}, u32[]{:S(2)}) %copy-start.1) | copy-done | bytes 294936
  13.6 1.1 %window_layout.1 = (bf16[8,128,256]{2,1,0:T(8,128)(2,1)S(1)}, bf16[128,2048]{1,0:T(8,128)(2,1)S(1)}, bf16[256,256]{1,0:T(8,128)(2,1)S(1)}, bf16[128,256]{1,0:T(8,128)(2,1)S(1)}, bf16[64,1152]{1,0:T(8,128)(2,1)S(1)}) custom-call(bf16[128,1152]{1,0:T(8,128)(2,1)S(1)} %copy-done.1, bf16[128,1152]{1,0:T(8,128)(2,1)S(1)} %copy-done, ...), custom_call_target="tpu_custom_call" | custom-call | bytes 2097152 | tf_op jit(solution)/shard_map/window_layout/pallas_call | solution.py:305
  14.6 0.6 %collective-permute-done.1.odd_up_ref = bf16[64,1152]{1,0:T(8,128)(2,1)S(1)} collective-permute-done((bf16[64,1152]{1,0:T(8,128)(2,1)S(1)}, bf16[64,1152]{1,0:T(8,128)(2,1)S(1)}, u32[]{:S(2)}, u32[]{:S(2)}) %collective-permute-start.1) | collective-permute-done | bytes 147488 | tf_op jit(solution)/shard_map/ppermute | solution.py:299
  15.2 0.0 collective-permute-done.2.even_up_ref
  15.2 0.9 %exchange_terms.1 = bf16[16,8,144]{2,1,0:T(8,128)(2,1)S(1)} custom-call(bf16[8,128,256]{2,1,0:T(8,128)(2,1)S(1)} %get-tuple-element.13.three_win, bf16[128,2048]{1,0:T(8,128)(2,1)S(1)} %get-tuple-element.14.metric_win, bf16[256,256]{1,0:T(8,128)(2,1)S(1)} %get-tuple-element.15.spread_win, bf16[128,256]{1,0:T(8,128)(2,1)S(1)} %get-tuple-element.16.kept_win, ...), custom_call_target="tpu_custom_call" | custom-call | flops 268435456 | bytes 2097152 | tf_op jit(solution)/shard_map/exchange_terms/pallas_call | solution.py:321
  16.1 15.9 %all_to_all.5 = bf16[16,8,144]{2,1,0:T(8,128)(2,1)S(1)} all-to-all(bf16[16,8,144]{2,1,0:T(8,128)(2,1)S(1)} %exchange_terms.1), channel_id=1, replica_groups={{13,0,1,2,3,4,5,6,7,8,9,10,11,12,14,15},{29,16,17,18,19,20,21,22,23,24,..., dimensions={0} | all-to-all | bytes 73728 | tf_op jit(solution)/shard_map/all_to_all | solution.py:330
  32.0 0.6 %reduce_sum.12 = bf16[8,144]{1,0:T(8,128)(2,1)} reduce(bf16[16,8,144]{2,1,0:T(8,128)(2,1)S(1)} %all_to_all.5, bf16[]{:T(256)} %constant.2.clone.1), dimensions={0}, to_apply=%region_0.0 | reduce | flops 17280 | bytes 39170 | tf_op jit(solution)/shard_map/reduce_sum | solution.py:331
Async XLA Ops:
  0.0 12.6 %copy-start = (bf16[128,1152]{1,0:T(8,128)(2,1)S(1)}, bf16[128,1152]{1,0:T(8,128)(2,1)}, u32[]{:S(2)}) copy-start(bf16[128,1152]{1,0:T(8,128)(2,1)} %metric_ref.1) | copy-start | bytes 884740
  0.0 12.6 %copy-start.2 = (bf16[128,144]{0,1:T(8,128)(2,1)S(1)}, bf16[128,144]{0,1:T(8,128)(2,1)}, u32[]{:S(2)}) copy-start(bf16[128,144]{0,1:T(8,128)(2,1)} %param.7) | copy-start | bytes 110596
  0.0 12.6 %copy-start.3 = (s32[8,9]{1,0:T(8,128)S(1)}, s32[8,9]{1,0:T(8,128)}, u32[]{:S(2)}) copy-start(s32[8,9]{1,0:T(8,128)} %pattern_ref.1) | copy-start | bytes 868
  1.3 11.3 %copy-start.4 = (s32[256]{0:T(256)S(1)}, s32[256]{0:T(256)}, u32[]{:S(2)}) copy-start(s32[256]{0:T(256)} %size_ref.1) | copy-start | bytes 3076
  1.3 11.3 %collective-permute-start = (bf16[64,1152]{1,0:T(8,128)(2,1)S(1)}, bf16[64,1152]{1,0:T(8,128)(2,1)S(1)}, u32[]{:S(2)}, u32[]{:S(2)}) collective-permute-start(bf16[64,1152]{1,0:T(8,128)(2,1)S(1)} %get-tuple-element.12), channel_id=1, source_target_pairs={{16,0},{336,320},{400,384},{464,448},{1,17},{17,1},{33,49},{49,33}... | collective-permute-start | bytes 442376 | tf_op jit(solution)/shard_map/ppermute | solution.py:299
  5.2 10.0 %collective-permute-start.1 = (bf16[64,1152]{1,0:T(8,128)(2,1)S(1)}, bf16[64,1152]{1,0:T(8,128)(2,1)S(1)}, u32[]{:S(2)}, u32[]{:S(2)}) collective-permute-start(bf16[64,1152]{1,0:T(8,128)(2,1)S(1)} %get-tuple-element.18), channel_id=1, source_target_pairs={{0,496},{16,32},{32,16},{48,64},{64,48},{80,96},{96,80},{112,128},... | collective-permute-start | bytes 442376 | tf_op jit(solution)/shard_map/ppermute | solution.py:299
  11.9 3.3 %collective-permute-start.2 = (bf16[64,1152]{1,0:T(8,128)(2,1)S(1)}, bf16[64,1152]{1,0:T(8,128)(2,1)S(1)}, u32[]{:S(2)}, u32[]{:S(2)}) collective-permute-start(bf16[64,1152]{1,0:T(8,128)(2,1)S(1)} %get-tuple-element.12), channel_id=1, source_target_pairs={{0,16},{32,48},{48,32},{64,80},{80,64},{96,112},{112,96},{128,144}... | collective-permute-start | bytes 442376 | tf_op jit(solution)/shard_map/ppermute | solution.py:299
  12.6 1.0 %copy-start.1 = (bf16[128,1152]{1,0:T(8,128)(2,1)S(1)}, bf16[128,1152]{1,0:T(8,128)(2,1)}, u32[]{:S(2)}) copy-start(bf16[128,1152]{1,0:T(8,128)(2,1)} %three_ref.1) | copy-start | bytes 884740

commit v6 on v5

--- a/solution.py
+++ b/solution.py
@@ -91,31 +91,32 @@
 
 
 def pack_halo(metric_ref, spread_ref, pattern_ref, sizes, up_ref, down_ref):
-    funcs = metric_ref.shape[1] // WIDTH
-    last = slice(funcs * LANES, (funcs + 1) * LANES)
+    lane = iota((BS, LANES), 1)
+    density = []
+    for g in range(PER):
+        slot_of, atom_of = {}, {}
+        for j in range(ATOMS):
+            at = g if j < HALF else g + ATOMS
+            if 0 <= at - j < SLOTS:
+                slot_of[j], atom_of[j] = at - j, at
+        density.append(density_rows(spread_ref, pattern_ref, sizes, slot_of, atom_of))
     for a in range(ATOMS):
         rows = slice(a * BS, (a + 1) * BS)
         first = 0 if a < HALF else ATOMS
         out_ref = down_ref if a < HALF else up_ref
         out_rows = slice((a % HALF) * BS, (a % HALF + 1) * BS)
         mask = row_mask(pattern_ref, sizes, a, first)
-        for p in range(funcs):
-            tile = banded(metric_ref, rows, p * WIDTH, (a - first) * BS, 1)[0]
-            out_ref[out_rows, p * LANES : (p + 1) * LANES] = tile * mask
-    lane = iota((BS, LANES), 1)
-    for g in range(HALF):
-        tiles = []
-        for c in (g, g + HALF):
-            slot_of, atom_of = {}, {}
-            for j in range(ATOMS):
-                at = c if j < HALF else c + ATOMS
-                if 0 <= at - j < SLOTS:
-                    slot_of[j], atom_of[j] = at - j, at
-            tiles.append(density_rows(spread_ref, pattern_ref, sizes, slot_of, atom_of))
-        near, far = tiles[0], pltpu.roll(tiles[1], LANES // 2, 1)
-        rows = slice(g * BS, (g + 1) * BS)
-        down_ref[rows, last] = jnp.where(lane < LANES // 2, near, far)
-        up_ref[rows, last] = jnp.where(lane < LANES // 2, far, near)
+        for p in range(PER):
+            tile = banded(metric_ref, rows, p * WIDTH, (a - first) * BS, 1)[0] * mask
+            if a == 2:
+                tile = jnp.where(lane < 16, pltpu.roll(density[p], 80, 1), tile)
+            elif a == 3:
+                tile = jnp.where(lane < 48, density[p], tile)
+            elif a == 4:
+                tile = jnp.where(lane >= 80, density[p], tile)
+            elif a == 5:
+                tile = jnp.where((lane >= 96) & (lane < 112), pltpu.roll(density[p], 32, 1), tile)
+            out_ref[out_rows, p * LANES : (p + 1) * LANES] = tile
 
 
 def pack_kernel(
@@ -197,34 +198,40 @@
 
 def main_kernel(place, three_win, metric_win, spread_win, kept_win, first_ref, odd_up_ref, even_up_ref, out_ref, spread_all):
     funcs = three_win.shape[0]
-    last = slice(funcs * LANES, (funcs + 1) * LANES)
-    low = iota((SIDE, LANES), 1) < LANES // 2
+    lane = iota((BS, LANES), 1)
     odd = lax.rem(lax.axis_index("orb"), 2) == 1
-
     here = lax.axis_index("orb")
     is_first = lax.rem(lax.axis_index("aux"), 2) == 1
     for target in AHEAD:
         is_first |= here == target
 
-    def even(cols):
-        return jnp.where(is_first, first_ref[:, cols], even_up_ref[:, cols])
-
-    def before(cols):
-        return jnp.where(odd, even(cols), odd_up_ref[:, cols])
-
-    def after(cols):
-        return jnp.where(odd, odd_up_ref[:, cols], even(cols))
-
+    def tiles_of(i, p):
+        place = slice(i * BS, (i + 1) * BS), slice(p * LANES, (p + 1) * LANES)
+        even = jnp.where(is_first, first_ref[place], even_up_ref[place])
+        other = odd_up_ref[place]
+        return jnp.where(odd, even, other), jnp.where(odd, other, even)
+
+    before, after = [], []
+    for i in range(HALF):
+        tiles = [tiles_of(i, p) for p in range(funcs)]
+        before.append([t[0] for t in tiles])
+        after.append([t[1] for t in tiles])
     spread_all[...] = spread_win[...]
-    for h in range(2):
-        tile = before(last)
-        tile = pltpu.roll(tile, LANES // 2, 1) if h == 0 else tile
-        rows = slice(h * SIDE, (h + 1) * SIDE)
-        spread_all[rows, :LANES] = jnp.where(low, tile, spread_win[rows, :LANES])
-        tile = after(last)
-        tile = pltpu.roll(tile, LANES // 2, 1) if h == 0 else tile
-        rows = slice((h + 2) * SIDE, (h + 3) * SIDE)
-        spread_all[rows, LANES:] = jnp.where(low, spread_win[rows, LANES:], tile)
+    for g in range(PER):
+        rows = slice(g * BS, (g + 1) * BS)
+        own = spread_win[rows, :LANES]
+        tile = jnp.where(lane < LANES // 2, pltpu.roll(before[0][g], 64, 1), own)
+        spread_all[rows, :LANES] = jnp.where(lane < BS, pltpu.roll(before[1][g], 32, 1), tile)
+        rows = slice((PER + g) * BS, (PER + g + 1) * BS)
+        own = spread_win[rows, LANES:]
+        tile = jnp.where(lane >= LANES // 2, pltpu.roll(after[3][g], 64, 1), own)
+        spread_all[rows, LANES:] = jnp.where(lane >= LANES - BS, pltpu.roll(after[2][g], 112, 1), tile)
+    zero = jnp.zeros((BS, LANES), jnp.bfloat16)
+    side_rows = []
+    for i in range(HALF):
+        side_rows.append([jnp.where(lane < (i + HALF + 1) * BS, t, zero) if i < 2 else t for t in before[i]])
+    for i in range(HALF):
+        side_rows.append([jnp.where(lane >= i * BS, t, zero) if i >= 2 else t for t in after[i]])
     atom = iota((ROWS, WINDOW), 0) // BS
     slot = iota((ROWS, WINDOW), 1) // BS - atom
     in_band = (slot >= 0) & (slot < SLOTS)
@@ -238,10 +245,9 @@
         jnp.concatenate(contracted, axis=1), metric_win[...], NT, preferred_element_type=jnp.float32
     )
     near = [jnp.concatenate([c[:SIDE, :LANES], c[SIDE:, LANES:]], axis=0) for c in contracted]
-    cols = slice(0, funcs * LANES)
     sides = lax.dot_general(
         jnp.concatenate(near, axis=1),
-        jnp.concatenate([before(cols), after(cols)], axis=0),
+        jnp.concatenate([jnp.concatenate(block, axis=1) for block in side_rows], axis=0),
         NT,
         preferred_element_type=jnp.float32,
     )
@@ -270,7 +276,7 @@
 def on_device(three_center, metric_tensor, density, pattern, block_size):
     funcs = three_center.shape[1] // WIDTH
     spread = density.T
-    message = pltpu.VMEM((SIDE, (funcs + 1) * LANES), jnp.bfloat16)
+    message = pltpu.VMEM((SIDE, funcs * LANES), jnp.bfloat16)
     odd_up, even_up = call(
         pack_kernel,
         (message, message),

time: 32.8 us -> 32.5 us (level)
  waiting for transfers between devices: 0.59 us -> 0.24 us
    ppermute x3, waiting for transfers between devices: 0.59 us -> 0.24 us  [swap(): return lax.ppermute(message, ('orb', 'aux'), pairs)]
where the time goes in v6:
time: 32.5 us; the launch traced here: 32.3 us
  blocking collectives  15.9 us (49%)
  starting transfers between devices  11.2 us (34%)
  Pallas kernels  3.2 us (10%)
  local copies, waits for them, and re-layouts  0.97 us (3%)
  other arithmetic  0.61 us (2%)
    all_to_all x1, blocking collectives, on_device(): terms = lax.all_to_all(partial_sum, 'aux', 0, 0, axis_index_groups=[order])  15.9 us
    ppermute x3, starting transfers between devices, swap(): return lax.ppermute(message, ('orb', 'aux'), pairs)  11.2 us
    pallas_call x1, Pallas kernels, on_device(): call(pack_kernel, (message, message), [HBM] * 4, 'pack_halo', 0, 1 << 20,...  1.27 us
    pallas_call x1, Pallas kernels, on_device(): call(prepare_kernel, (wide, jax.ShapeDtypeStruct((ROWS, funcs * WINDOW),...  1.05 us
    unnamed x10, local copies, waits for them, and re-layouts  0.97 us
    pallas_call x1, Pallas kernels, on_device(): call(functools.partial(main_kernel, [order.index(i) for i in range(funcs_...  0.87 us
  transfers between devices with their start and end apart: 3, of which 1 were waited for; matrix products, arithmetic and copies ran while one was open for 0% of the time, Pallas kernels for 3%

profile of v6, /device:TPU:1, one launch (start us, length us, event | category | flops | bytes accessed | tf_op | source)
XLA Modules:
  0.0 32.3 jit_solution(8621396411937798470)
XLA Ops:
  0.0 0.0 copy-start
  0.0 0.0 copy-start.2
  0.0 0.0 copy-start.3
  0.0 1.3 %pack_halo.1 = (bf16[64,1024]{1,0:T(8,128)(2,1)S(1)}, bf16[64,1024]{1,0:T(8,128)(2,1)S(1)}) custom-call(bf16[128,1152]{1,0:T(8,128)(2,1)} %metric_ref.1, bf16[144,128]{1,0:T(8,128)(2,1)} %bitcast.1, s32[8,9]{1,0:T(8,128)} %pattern_ref.1, s32[256]{0:T(256)} %size_ref.1), custom_call_target="tpu_custom_call" | custom-call | bytes 1048576 | tf_op jit(solution)/shard_map/pack_halo/pallas_call | solution.py:280
  1.3 0.0 copy-start.4
  1.3 4.0 %collective-permute-start = (bf16[64,1024]{1,0:T(8,128)(2,1)S(1)}, bf16[64,1024]{1,0:T(8,128)(2,1)S(1)}, u32[]{:S(2)}, u32[]{:S(2)}) collective-permute-start(bf16[64,1024]{1,0:T(8,128)(2,1)S(1)} %get-tuple-element.12), channel_id=1, source_target_pairs={{16,0},{336,320},{400,384},{464,448},{1,17},{17,1},{33,49},{49,33}... | collective-permute-start | bytes 393224 | tf_op jit(solution)/shard_map/ppermute | solution.py:305
  5.3 6.6 %collective-permute-start.1 = (bf16[64,1024]{1,0:T(8,128)(2,1)S(1)}, bf16[64,1024]{1,0:T(8,128)(2,1)S(1)}, u32[]{:S(2)}, u32[]{:S(2)}) collective-permute-start(bf16[64,1024]{1,0:T(8,128)(2,1)S(1)} %get-tuple-element.18), channel_id=1, source_target_pairs={{0,496},{16,32},{32,16},{48,64},{64,48},{80,96},{96,80},{112,128},... | collective-permute-start | bytes 393224 | tf_op jit(solution)/shard_map/ppermute | solution.py:305
  11.9 0.7 %collective-permute-start.2 = (bf16[64,1024]{1,0:T(8,128)(2,1)S(1)}, bf16[64,1024]{1,0:T(8,128)(2,1)S(1)}, u32[]{:S(2)}, u32[]{:S(2)}) collective-permute-start(bf16[64,1024]{1,0:T(8,128)(2,1)S(1)} %get-tuple-element.12), channel_id=1, source_target_pairs={{0,16},{32,48},{48,32},{64,80},{80,64},{96,112},{112,96},{128,144}... | collective-permute-start | bytes 393224 | tf_op jit(solution)/shard_map/ppermute | solution.py:305
  12.6 0.0 collective-permute-done.message_ref
  12.6 0.0 copy-done
  12.6 0.0 copy-done.2
  12.6 0.0 copy-done.3
  12.6 0.0 copy-done.4
  12.6 0.0 copy-start.1
  12.6 1.0 %copy-done.1 = bf16[128,1152]{1,0:T(8,128)(2,1)S(1)} copy-done((bf16[128,1152]{1,0:T(8,128)(2,1)S(1)}, bf16[128,1152]{1,0:T(8,128)(2,1)}, u32[]{:S(2)}) %copy-start.1) | copy-done | bytes 294936
  13.6 1.1 %window_layout.1 = (bf16[8,128,256]{2,1,0:T(8,128)(2,1)S(1)}, bf16[128,2048]{1,0:T(8,128)(2,1)S(1)}, bf16[256,256]{1,0:T(8,128)(2,1)S(1)}, bf16[128,256]{1,0:T(8,128)(2,1)S(1)}, bf16[64,1024]{1,0:T(8,128)(2,1)S(1)}) custom-call(bf16[128,1152]{1,0:T(8,128)(2,1)S(1)} %copy-done.1, bf16[128,1152]{1,0:T(8,128)(2,1)S(1)} %copy-done, ...), custom_call_target="tpu_custom_call" | custom-call | bytes 2097152 | tf_op jit(solution)/shard_map/window_layout/pallas_call | solution.py:311
  14.6 0.2 collective-permute-done.1.odd_up_ref
  14.9 0.0 collective-permute-done.2.even_up_ref
  14.9 0.9 %exchange_terms.1 = bf16[16,8,144]{2,1,0:T(8,128)(2,1)S(1)} custom-call(bf16[8,128,256]{2,1,0:T(8,128)(2,1)S(1)} %get-tuple-element.13.three_win, bf16[128,2048]{1,0:T(8,128)(2,1)S(1)} %get-tuple-element.14.metric_win, bf16[256,256]{1,0:T(8,128)(2,1)S(1)} %get-tuple-element.15.spread_win, bf16[128,256]{1,0:T(8,128)(2,1)S(1)} %get-tuple-element.16.kept_win, ...), custom_call_target="tpu_custom_call" | custom-call | flops 268435456 | bytes 2097152 | tf_op jit(solution)/shard_map/exchange_terms/pallas_call | solution.py:327
  15.8 15.9 %all_to_all.5 = bf16[16,8,144]{2,1,0:T(8,128)(2,1)S(1)} all-to-all(bf16[16,8,144]{2,1,0:T(8,128)(2,1)S(1)} %exchange_terms.1), channel_id=1, replica_groups={{13,0,1,2,3,4,5,6,7,8,9,10,11,12,14,15},{29,16,17,18,19,20,21,22,23,24,..., dimensions={0} | all-to-all | bytes 73728 | tf_op jit(solution)/shard_map/all_to_all | solution.py:336
  31.7 0.6 %reduce_sum.12 = bf16[8,144]{1,0:T(8,128)(2,1)} reduce(bf16[16,8,144]{2,1,0:T(8,128)(2,1)S(1)} %all_to_all.5, bf16[]{:T(256)} %constant.2.clone.1), dimensions={0}, to_apply=%region_0.0 | reduce | flops 17280 | bytes 39170 | tf_op jit(solution)/shard_map/reduce_sum | solution.py:337
Async XLA Ops:
  0.0 12.6 %copy-start = (bf16[128,1152]{1,0:T(8,128)(2,1)S(1)}, bf16[128,1152]{1,0:T(8,128)(2,1)}, u32[]{:S(2)}) copy-start(bf16[128,1152]{1,0:T(8,128)(2,1)} %metric_ref.1) | copy-start | bytes 884740
  0.0 12.6 %copy-start.2 = (bf16[128,144]{0,1:T(8,128)(2,1)S(1)}, bf16[128,144]{0,1:T(8,128)(2,1)}, u32[]{:S(2)}) copy-start(bf16[128,144]{0,1:T(8,128)(2,1)} %param.7) | copy-start | bytes 110596
  0.0 12.6 %copy-start.3 = (s32[8,9]{1,0:T(8,128)S(1)}, s32[8,9]{1,0:T(8,128)}, u32[]{:S(2)}) copy-start(s32[8,9]{1,0:T(8,128)} %pattern_ref.1) | copy-start | bytes 868
  1.3 11.3 %copy-start.4 = (s32[256]{0:T(256)S(1)}, s32[256]{0:T(256)}, u32[]{:S(2)}) copy-start(s32[256]{0:T(256)} %size_ref.1) | copy-start | bytes 3076
  1.3 11.3 %collective-permute-start = (bf16[64,1024]{1,0:T(8,128)(2,1)S(1)}, bf16[64,1024]{1,0:T(8,128)(2,1)S(1)}, u32[]{:S(2)}, u32[]{:S(2)}) collective-permute-start(bf16[64,1024]{1,0:T(8,128)(2,1)S(1)} %get-tuple-element.12), channel_id=1, source_target_pairs={{16,0},{336,320},{400,384},{464,448},{1,17},{17,1},{33,49},{49,33}... | collective-permute-start | bytes 393224 | tf_op jit(solution)/shard_map/ppermute | solution.py:305
  5.3 9.6 %collective-permute-start.1 = (bf16[64,1024]{1,0:T(8,128)(2,1)S(1)}, bf16[64,1024]{1,0:T(8,128)(2,1)S(1)}, u32[]{:S(2)}, u32[]{:S(2)}) collective-permute-start(bf16[64,1024]{1,0:T(8,128)(2,1)S(1)} %get-tuple-element.18), channel_id=1, source_target_pairs={{0,496},{16,32},{32,16},{48,64},{64,48},{80,96},{96,80},{112,128},... | collective-permute-start | bytes 393224 | tf_op jit(solution)/shard_map/ppermute | solution.py:305
  11.9 3.0 %collective-permute-start.2 = (bf16[64,1024]{1,0:T(8,128)(2,1)S(1)}, bf16[64,1024]{1,0:T(8,128)(2,1)S(1)}, u32[]{:S(2)}, u32[]{:S(2)}) collective-permute-start(bf16[64,1024]{1,0:T(8,128)(2,1)S(1)} %get-tuple-element.12), channel_id=1, source_target_pairs={{0,16},{32,48},{48,32},{64,80},{80,64},{96,112},{112,96},{128,144}... | collective-permute-start | bytes 393224 | tf_op jit(solution)/shard_map/ppermute | solution.py:305
  12.6 1.0 %copy-start.1 = (bf16[128,1152]{1,0:T(8,128)(2,1)S(1)}, bf16[128,1152]{1,0:T(8,128)(2,1)}, u32[]{:S(2)}) copy-start(bf16[128,1152]{1,0:T(8,128)(2,1)} %three_ref.1) | copy-start | bytes 884740

commit v7 on v6

--- a/solution.py
+++ b/solution.py
@@ -201,7 +201,7 @@
     lane = iota((BS, LANES), 1)
     odd = lax.rem(lax.axis_index("orb"), 2) == 1
     here = lax.axis_index("orb")
-    is_first = lax.rem(lax.axis_index("aux"), 2) == 1
+    is_first = (lax.rem(lax.axis_index("aux"), 2) == 1) & (here < lax.axis_size("orb") - 2)
     for target in AHEAD:
         is_first |= here == target
 
@@ -304,9 +304,10 @@
         ]
         return lax.ppermute(message, ("orb", "aux"), pairs)
 
-    from_first_even = swap(even_up, ahead, even_pairs)
+    late = [(i, j) for i, j in even_pairs if peers - 1 in (i, j)]
+    from_first_even = swap(even_up, ahead, [p for p in even_pairs if p not in late])
     from_odd_up = swap(odd_up, odd_pairs, odd_pairs)
-    from_even_up = swap(even_up, behind, [])
+    from_even_up = swap(even_up, behind, late)
     wide = jax.ShapeDtypeStruct((funcs, ROWS, WINDOW), jnp.bfloat16)
     prepared = call(
         prepare_kernel,

time: 32.5 us -> 32.5 us (level)
  starting transfers between devices: 11.2 us -> 9.46 us
  waiting for transfers between devices: 0.24 us -> 1.44 us
  blocking collectives: 15.9 us -> 16.5 us
    ppermute x3, starting transfers between devices: 11.2 us -> 9.46 us  [swap(): return lax.ppermute(message, ('orb', 'aux'), pairs)]
    ppermute x3, waiting for transfers between devices: 0.24 us -> 1.44 us  [swap(): return lax.ppermute(message, ('orb', 'aux'), pairs)]
    all_to_all x1, blocking collectives: 15.9 us -> 16.5 us  [on_device(): terms = lax.all_to_all(partial_sum, 'aux', 0, 0, axis_index_groups=[order])]
where the time goes in v7:
time: 32.5 us; the launch traced here: 32.3 us
  blocking collectives  16.5 us (51%)
  starting transfers between devices  9.46 us (29%)
  Pallas kernels  3.2 us (10%)
  waiting for transfers between devices  1.44 us (4%)
  local copies, waits for them, and re-layouts  0.97 us (3%)
  other arithmetic  0.61 us (2%)
    all_to_all x1, blocking collectives, on_device(): terms = lax.all_to_all(partial_sum, 'aux', 0, 0, axis_index_groups=[order])  16.5 us
    ppermute x3, starting transfers between devices, swap(): return lax.ppermute(message, ('orb', 'aux'), pairs)  9.46 us
    ppermute x3, waiting for transfers between devices, swap(): return lax.ppermute(message, ('orb', 'aux'), pairs)  1.44 us
    pallas_call x1, Pallas kernels, on_device(): call(pack_kernel, (message, message), [HBM] * 4, 'pack_halo', 0, 1 << 20,...  1.27 us
    pallas_call x1, Pallas kernels, on_device(): call(prepare_kernel, (wide, jax.ShapeDtypeStruct((ROWS, funcs * WINDOW),...  1.05 us
    unnamed x10, local copies, waits for them, and re-layouts  0.97 us
    pallas_call x1, Pallas kernels, on_device(): call(functools.partial(main_kernel, [order.index(i) for i in range(funcs_...  0.87 us
  transfers between devices with their start and end apart: 3, of which 1 were waited for; matrix products, arithmetic and copies ran while one was open for 0% of the time, Pallas kernels for 3%

profile of v7, /device:TPU:1, one launch (start us, length us, event | category | flops | bytes accessed | tf_op | source)
XLA Modules:
  0.0 32.3 jit_solution(10296511590051927278)
XLA Ops:
  0.0 0.0 copy-start
  0.0 0.0 copy-start.2
  0.0 0.0 copy-start.3
  0.0 1.3 %pack_halo.1 = (bf16[64,1024]{1,0:T(8,128)(2,1)S(1)}, bf16[64,1024]{1,0:T(8,128)(2,1)S(1)}) custom-call(bf16[128,1152]{1,0:T(8,128)(2,1)} %metric_ref.1, bf16[144,128]{1,0:T(8,128)(2,1)} %bitcast.1, s32[8,9]{1,0:T(8,128)} %pattern_ref.1, s32[256]{0:T(256)} %size_ref.1), custom_call_target="tpu_custom_call" | custom-call | bytes 1048576 | tf_op jit(solution)/shard_map/pack_halo/pallas_call | solution.py:280
  1.3 0.0 copy-start.4
  1.3 4.0 %collective-permute-start = (bf16[64,1024]{1,0:T(8,128)(2,1)S(1)}, bf16[64,1024]{1,0:T(8,128)(2,1)S(1)}, u32[]{:S(2)}, u32[]{:S(2)}) collective-permute-start(bf16[64,1024]{1,0:T(8,128)(2,1)S(1)} %get-tuple-element.12), channel_id=1, source_target_pairs={{16,0},{336,320},{400,384},{464,448},{1,17},{17,1},{33,49},{49,33}... | collective-permute-start | bytes 393224 | tf_op jit(solution)/shard_map/ppermute | solution.py:305
  5.3 4.8 %collective-permute-start.1 = (bf16[64,1024]{1,0:T(8,128)(2,1)S(1)}, bf16[64,1024]{1,0:T(8,128)(2,1)S(1)}, u32[]{:S(2)}, u32[]{:S(2)}) collective-permute-start(bf16[64,1024]{1,0:T(8,128)(2,1)S(1)} %get-tuple-element.18), channel_id=1, source_target_pairs={{0,496},{16,32},{32,16},{48,64},{64,48},{80,96},{96,80},{112,128},... | collective-permute-start | bytes 393224 | tf_op jit(solution)/shard_map/ppermute | solution.py:305
  10.1 0.7 %collective-permute-start.2 = (bf16[64,1024]{1,0:T(8,128)(2,1)S(1)}, bf16[64,1024]{1,0:T(8,128)(2,1)S(1)}, u32[]{:S(2)}, u32[]{:S(2)}) collective-permute-start(bf16[64,1024]{1,0:T(8,128)(2,1)S(1)} %get-tuple-element.12), channel_id=1, source_target_pairs={{0,16},{32,48},{48,32},{64,80},{80,64},{96,112},{112,96},{128,144}... | collective-permute-start | bytes 393224 | tf_op jit(solution)/shard_map/ppermute | solution.py:305
  10.8 0.0 collective-permute-done.message_ref
  10.8 0.0 copy-done
  10.8 0.0 copy-done.2
  10.8 0.0 copy-done.3
  10.8 0.0 copy-done.4
  10.8 0.0 copy-start.1
  10.8 1.0 %copy-done.1 = bf16[128,1152]{1,0:T(8,128)(2,1)S(1)} copy-done((bf16[128,1152]{1,0:T(8,128)(2,1)S(1)}, bf16[128,1152]{1,0:T(8,128)(2,1)}, u32[]{:S(2)}) %copy-start.1) | copy-done | bytes 294936
  11.8 1.1 %window_layout.1 = (bf16[8,128,256]{2,1,0:T(8,128)(2,1)S(1)}, bf16[128,2048]{1,0:T(8,128)(2,1)S(1)}, bf16[256,256]{1,0:T(8,128)(2,1)S(1)}, bf16[128,256]{1,0:T(8,128)(2,1)S(1)}, bf16[64,1024]{1,0:T(8,128)(2,1)S(1)}) custom-call(bf16[128,1152]{1,0:T(8,128)(2,1)S(1)} %copy-done.1, bf16[128,1152]{1,0:T(8,128)(2,1)S(1)} %copy-done, ...), custom_call_target="tpu_custom_call" | custom-call | bytes 2097152 | tf_op jit(solution)/shard_map/window_layout/pallas_call | solution.py:312
  12.9 1.4 %collective-permute-done.1.odd_up_ref = bf16[64,1024]{1,0:T(8,128)(2,1)S(1)} collective-permute-done((bf16[64,1024]{1,0:T(8,128)(2,1)S(1)}, bf16[64,1024]{1,0:T(8,128)(2,1)S(1)}, u32[]{:S(2)}, u32[]{:S(2)}) %collective-permute-start.1) | collective-permute-done | bytes 131104 | tf_op jit(solution)/shard_map/ppermute | solution.py:305
  14.3 0.0 collective-permute-done.2.even_up_ref
  14.3 0.9 %exchange_terms.1 = bf16[16,8,144]{2,1,0:T(8,128)(2,1)S(1)} custom-call(bf16[8,128,256]{2,1,0:T(8,128)(2,1)S(1)} %get-tuple-element.13.three_win, bf16[128,2048]{1,0:T(8,128)(2,1)S(1)} %get-tuple-element.14.metric_win, bf16[256,256]{1,0:T(8,128)(2,1)S(1)} %get-tuple-element.15.spread_win, bf16[128,256]{1,0:T(8,128)(2,1)S(1)} %get-tuple-element.16.kept_win, ...), custom_call_target="tpu_custom_call" | custom-call | flops 268435456 | bytes 2097152 | tf_op jit(solution)/shard_map/exchange_terms/pallas_call | solution.py:328
  15.2 16.5 %all_to_all.5 = bf16[16,8,144]{2,1,0:T(8,128)(2,1)S(1)} all-to-all(bf16[16,8,144]{2,1,0:T(8,128)(2,1)S(1)} %exchange_terms.1), channel_id=1, replica_groups={{13,0,1,2,3,4,5,6,7,8,9,10,11,12,14,15},{29,16,17,18,19,20,21,22,23,24,..., dimensions={0} | all-to-all | bytes 73728 | tf_op jit(solution)/shard_map/all_to_all | solution.py:337
  31.7 0.6 %reduce_sum.12 = bf16[8,144]{1,0:T(8,128)(2,1)} reduce(bf16[16,8,144]{2,1,0:T(8,128)(2,1)S(1)} %all_to_all.5, bf16[]{:T(256)} %constant.2.clone.1), dimensions={0}, to_apply=%region_0.0 | reduce | flops 17280 | bytes 39170 | tf_op jit(solution)/shard_map/reduce_sum | solution.py:338
Async XLA Ops:
  0.0 10.8 %copy-start = (bf16[128,1152]{1,0:T(8,128)(2,1)S(1)}, bf16[128,1152]{1,0:T(8,128)(2,1)}, u32[]{:S(2)}) copy-start(bf16[128,1152]{1,0:T(8,128)(2,1)} %metric_ref.1) | copy-start | bytes 884740
  0.0 10.8 %copy-start.2 = (bf16[128,144]{0,1:T(8,128)(2,1)S(1)}, bf16[128,144]{0,1:T(8,128)(2,1)}, u32[]{:S(2)}) copy-start(bf16[128,144]{0,1:T(8,128)(2,1)} %param.7) | copy-start | bytes 110596
  0.0 10.8 %copy-start.3 = (s32[8,9]{1,0:T(8,128)S(1)}, s32[8,9]{1,0:T(8,128)}, u32[]{:S(2)}) copy-start(s32[8,9]{1,0:T(8,128)} %pattern_ref.1) | copy-start | bytes 868
  1.3 9.5 %copy-start.4 = (s32[256]{0:T(256)S(1)}, s32[256]{0:T(256)}, u32[]{:S(2)}) copy-start(s32[256]{0:T(256)} %size_ref.1) | copy-start | bytes 3076
  1.3 9.5 %collective-permute-start = (bf16[64,1024]{1,0:T(8,128)(2,1)S(1)}, bf16[64,1024]{1,0:T(8,128)(2,1)S(1)}, u32[]{:S(2)}, u32[]{:S(2)}) collective-permute-start(bf16[64,1024]{1,0:T(8,128)(2,1)S(1)} %get-tuple-element.12), channel_id=1, source_target_pairs={{16,0},{336,320},{400,384},{464,448},{1,17},{17,1},{33,49},{49,33}... | collective-permute-start | bytes 393224 | tf_op jit(solution)/shard_map/ppermute | solution.py:305
  5.3 9.0 %collective-permute-start.1 = (bf16[64,1024]{1,0:T(8,128)(2,1)S(1)}, bf16[64,1024]{1,0:T(8,128)(2,1)S(1)}, u32[]{:S(2)}, u32[]{:S(2)}) collective-permute-start(bf16[64,1024]{1,0:T(8,128)(2,1)S(1)} %get-tuple-element.18), channel_id=1, source_target_pairs={{0,496},{16,32},{32,16},{48,64},{64,48},{80,96},{96,80},{112,128},... | collective-permute-start | bytes 393224 | tf_op jit(solution)/shard_map/ppermute | solution.py:305
  10.1 4.2 %collective-permute-start.2 = (bf16[64,1024]{1,0:T(8,128)(2,1)S(1)}, bf16[64,1024]{1,0:T(8,128)(2,1)S(1)}, u32[]{:S(2)}, u32[]{:S(2)}) collective-permute-start(bf16[64,1024]{1,0:T(8,128)(2,1)S(1)} %get-tuple-element.12), channel_id=1, source_target_pairs={{0,16},{32,48},{48,32},{64,80},{80,64},{96,112},{112,96},{128,144}... | collective-permute-start | bytes 393224 | tf_op jit(solution)/shard_map/ppermute | solution.py:305
  10.8 1.0 %copy-start.1 = (bf16[128,1152]{1,0:T(8,128)(2,1)S(1)}, bf16[128,1152]{1,0:T(8,128)(2,1)}, u32[]{:S(2)}) copy-start(bf16[128,1152]{1,0:T(8,128)(2,1)} %three_ref.1) | copy-start | bytes 884740

commit v8 on v6

--- a/solution.py
+++ b/solution.py
@@ -322,7 +322,7 @@
         0,
         2 << 20,
     )(three_center, metric_tensor, spread, pattern, block_size, from_first_even)
-    lead = funcs_at - 3
+    lead = funcs_at - 5
     order = [lead] + [i for i in range(funcs_at) if i != lead]
     partial_sum = call(
         functools.partial(main_kernel, [order.index(i) for i in range(funcs_at)]),

time: 32.5 us -> 32.4 us (level)
  no operation moved by 1% of the time
where the time goes in v8:
time: 32.4 us; the launch traced here: 32.2 us
  blocking collectives  15.8 us (49%)
  starting transfers between devices  11.2 us (35%)
  Pallas kernels  3.2 us (10%)
  local copies, waits for them, and re-layouts  0.97 us (3%)
  other arithmetic  0.61 us (2%)
    all_to_all x1, blocking collectives, on_device(): terms = lax.all_to_all(partial_sum, 'aux', 0, 0, axis_index_groups=[order])  15.8 us
    ppermute x3, starting transfers between devices, swap(): return lax.ppermute(message, ('orb', 'aux'), pairs)  11.2 us
    pallas_call x1, Pallas kernels, on_device(): call(pack_kernel, (message, message), [HBM] * 4, 'pack_halo', 0, 1 << 20,...  1.27 us
    pallas_call x1, Pallas kernels, on_device(): call(prepare_kernel, (wide, jax.ShapeDtypeStruct((ROWS, funcs * WINDOW),...  1.05 us
    unnamed x10, local copies, waits for them, and re-layouts  0.97 us
    pallas_call x1, Pallas kernels, on_device(): call(functools.partial(main_kernel, [order.index(i) for i in range(funcs_...  0.87 us
  transfers between devices with their start and end apart: 3, of which 1 were waited for; matrix products, arithmetic and copies ran while one was open for 0% of the time, Pallas kernels for 3%

profile of v8, /device:TPU:1, one launch (start us, length us, event | category | flops | bytes accessed | tf_op | source)
XLA Modules:
  0.0 32.2 jit_solution(5540165067873657211)
XLA Ops:
  0.0 0.0 copy-start
  0.0 0.0 copy-start.2
  0.0 0.0 copy-start.3
  0.0 1.3 %pack_halo.1 = (bf16[64,1024]{1,0:T(8,128)(2,1)S(1)}, bf16[64,1024]{1,0:T(8,128)(2,1)S(1)}) custom-call(bf16[128,1152]{1,0:T(8,128)(2,1)} %metric_ref.1, bf16[144,128]{1,0:T(8,128)(2,1)} %bitcast.1, s32[8,9]{1,0:T(8,128)} %pattern_ref.1, s32[256]{0:T(256)} %size_ref.1), custom_call_target="tpu_custom_call" | custom-call | bytes 1048576 | tf_op jit(solution)/shard_map/pack_halo/pallas_call | solution.py:280
  1.3 0.0 copy-start.4
  1.3 4.0 %collective-permute-start = (bf16[64,1024]{1,0:T(8,128)(2,1)S(1)}, bf16[64,1024]{1,0:T(8,128)(2,1)S(1)}, u32[]{:S(2)}, u32[]{:S(2)}) collective-permute-start(bf16[64,1024]{1,0:T(8,128)(2,1)S(1)} %get-tuple-element.12), channel_id=1, source_target_pairs={{16,0},{336,320},{400,384},{464,448},{1,17},{17,1},{33,49},{49,33}... | collective-permute-start | bytes 393224 | tf_op jit(solution)/shard_map/ppermute | solution.py:305
  5.3 6.6 %collective-permute-start.1 = (bf16[64,1024]{1,0:T(8,128)(2,1)S(1)}, bf16[64,1024]{1,0:T(8,128)(2,1)S(1)}, u32[]{:S(2)}, u32[]{:S(2)}) collective-permute-start(bf16[64,1024]{1,0:T(8,128)(2,1)S(1)} %get-tuple-element.18), channel_id=1, source_target_pairs={{0,496},{16,32},{32,16},{48,64},{64,48},{80,96},{96,80},{112,128},... | collective-permute-start | bytes 393224 | tf_op jit(solution)/shard_map/ppermute | solution.py:305
  11.9 0.7 %collective-permute-start.2 = (bf16[64,1024]{1,0:T(8,128)(2,1)S(1)}, bf16[64,1024]{1,0:T(8,128)(2,1)S(1)}, u32[]{:S(2)}, u32[]{:S(2)}) collective-permute-start(bf16[64,1024]{1,0:T(8,128)(2,1)S(1)} %get-tuple-element.12), channel_id=1, source_target_pairs={{0,16},{32,48},{48,32},{64,80},{80,64},{96,112},{112,96},{128,144}... | collective-permute-start | bytes 393224 | tf_op jit(solution)/shard_map/ppermute | solution.py:305
  12.6 0.0 collective-permute-done.message_ref
  12.6 0.0 copy-done
  12.6 0.0 copy-done.2
  12.6 0.0 copy-done.3
  12.6 0.0 copy-done.4
  12.6 0.0 copy-start.1
  12.6 1.0 %copy-done.1 = bf16[128,1152]{1,0:T(8,128)(2,1)S(1)} copy-done((bf16[128,1152]{1,0:T(8,128)(2,1)S(1)}, bf16[128,1152]{1,0:T(8,128)(2,1)}, u32[]{:S(2)}) %copy-start.1) | copy-done | bytes 294936
  13.6 1.1 %window_layout.1 = (bf16[8,128,256]{2,1,0:T(8,128)(2,1)S(1)}, bf16[128,2048]{1,0:T(8,128)(2,1)S(1)}, bf16[256,256]{1,0:T(8,128)(2,1)S(1)}, bf16[128,256]{1,0:T(8,128)(2,1)S(1)}, bf16[64,1024]{1,0:T(8,128)(2,1)S(1)}) custom-call(bf16[128,1152]{1,0:T(8,128)(2,1)S(1)} %copy-done.1, bf16[128,1152]{1,0:T(8,128)(2,1)S(1)} %copy-done, ...), custom_call_target="tpu_custom_call" | custom-call | bytes 2097152 | tf_op jit(solution)/shard_map/window_layout/pallas_call | solution.py:311
  14.6 0.2 collective-permute-done.1.odd_up_ref
  14.9 0.0 collective-permute-done.2.even_up_ref
  14.9 0.9 %exchange_terms.1 = bf16[16,8,144]{2,1,0:T(8,128)(2,1)S(1)} custom-call(bf16[8,128,256]{2,1,0:T(8,128)(2,1)S(1)} %get-tuple-element.13.three_win, bf16[128,2048]{1,0:T(8,128)(2,1)S(1)} %get-tuple-element.14.metric_win, bf16[256,256]{1,0:T(8,128)(2,1)S(1)} %get-tuple-element.15.spread_win, bf16[128,256]{1,0:T(8,128)(2,1)S(1)} %get-tuple-element.16.kept_win, ...), custom_call_target="tpu_custom_call" | custom-call | flops 268435456 | bytes 2097152 | tf_op jit(solution)/shard_map/exchange_terms/pallas_call | solution.py:327
  15.8 15.8 %all_to_all.5 = bf16[16,8,144]{2,1,0:T(8,128)(2,1)S(1)} all-to-all(bf16[16,8,144]{2,1,0:T(8,128)(2,1)S(1)} %exchange_terms.1), channel_id=1, replica_groups={{11,0,1,2,3,4,5,6,7,8,9,10,12,13,14,15},{27,16,17,18,19,20,21,22,23,24,..., dimensions={0} | all-to-all | bytes 73728 | tf_op jit(solution)/shard_map/all_to_all | solution.py:336
  31.6 0.6 %reduce_sum.12 = bf16[8,144]{1,0:T(8,128)(2,1)} reduce(bf16[16,8,144]{2,1,0:T(8,128)(2,1)S(1)} %all_to_all.5, bf16[]{:T(256)} %constant.2.clone.1), dimensions={0}, to_apply=%region_0.0 | reduce | flops 17280 | bytes 39170 | tf_op jit(solution)/shard_map/reduce_sum | solution.py:337
Async XLA Ops:
  0.0 12.6 %copy-start = (bf16[128,1152]{1,0:T(8,128)(2,1)S(1)}, bf16[128,1152]{1,0:T(8,128)(2,1)}, u32[]{:S(2)}) copy-start(bf16[128,1152]{1,0:T(8,128)(2,1)} %metric_ref.1) | copy-start | bytes 884740
  0.0 12.6 %copy-start.2 = (bf16[128,144]{0,1:T(8,128)(2,1)S(1)}, bf16[128,144]{0,1:T(8,128)(2,1)}, u32[]{:S(2)}) copy-start(bf16[128,144]{0,1:T(8,128)(2,1)} %param.7) | copy-start | bytes 110596
  0.0 12.6 %copy-start.3 = (s32[8,9]{1,0:T(8,128)S(1)}, s32[8,9]{1,0:T(8,128)}, u32[]{:S(2)}) copy-start(s32[8,9]{1,0:T(8,128)} %pattern_ref.1) | copy-start | bytes 868
  1.3 11.3 %copy-start.4 = (s32[256]{0:T(256)S(1)}, s32[256]{0:T(256)}, u32[]{:S(2)}) copy-start(s32[256]{0:T(256)} %size_ref.1) | copy-start | bytes 3076
  1.3 11.3 %collective-permute-start = (bf16[64,1024]{1,0:T(8,128)(2,1)S(1)}, bf16[64,1024]{1,0:T(8,128)(2,1)S(1)}, u32[]{:S(2)}, u32[]{:S(2)}) collective-permute-start(bf16[64,1024]{1,0:T(8,128)(2,1)S(1)} %get-tuple-element.12), channel_id=1, source_target_pairs={{16,0},{336,320},{400,384},{464,448},{1,17},{17,1},{33,49},{49,33}... | collective-permute-start | bytes 393224 | tf_op jit(solution)/shard_map/ppermute | solution.py:305
  5.3 9.6 %collective-permute-start.1 = (bf16[64,1024]{1,0:T(8,128)(2,1)S(1)}, bf16[64,1024]{1,0:T(8,128)(2,1)S(1)}, u32[]{:S(2)}, u32[]{:S(2)}) collective-permute-start(bf16[64,1024]{1,0:T(8,128)(2,1)S(1)} %get-tuple-element.18), channel_id=1, source_target_pairs={{0,496},{16,32},{32,16},{48,64},{64,48},{80,96},{96,80},{112,128},... | collective-permute-start | bytes 393224 | tf_op jit(solution)/shard_map/ppermute | solution.py:305
  11.9 3.0 %collective-permute-start.2 = (bf16[64,1024]{1,0:T(8,128)(2,1)S(1)}, bf16[64,1024]{1,0:T(8,128)(2,1)S(1)}, u32[]{:S(2)}, u32[]{:S(2)}) collective-permute-start(bf16[64,1024]{1,0:T(8,128)(2,1)S(1)} %get-tuple-element.12), channel_id=1, source_target_pairs={{0,16},{32,48},{48,32},{64,80},{80,64},{96,112},{112,96},{128,144}... | collective-permute-start | bytes 393224 | tf_op jit(solution)/shard_map/ppermute | solution.py:305
  12.6 1.0 %copy-start.1 = (bf16[128,1152]{1,0:T(8,128)(2,1)S(1)}, bf16[128,1152]{1,0:T(8,128)(2,1)}, u32[]{:S(2)}) copy-start(bf16[128,1152]{1,0:T(8,128)(2,1)} %three_ref.1) | copy-start | bytes 884740
